TPU v7x, 256 devices: a whole 4x4x8 slice. The times are simulated.
256 devices in a mesh: ctx: 32 (over x_hi, z, core), head: 8 (over x_lo, y).
Axes of the slice: x: 4 (x_hi: 2, x_lo: 2; x = x_hi * 2 + x_lo), y: 4, z: 8, core: 2. Of those that a mesh axis runs over, the one named last changes fastest.
Arguments:
- queries: bfloat16 [4096, 2048], P('ctx', 'head'), may hold values from -6 to 6
- key_rows: bfloat16 [4096, 2048], P('ctx', 'head'), may hold values from -6 to 6
- value_rows: bfloat16 [4096, 2048], P('ctx', 'head'), may hold values from -13 to 13
- output_weight: bfloat16 [2048, 2048], P('head'), may hold values from -1 to 1
- residual_stream: bfloat16 [4096, 2048], P('ctx', 'head'), may hold values from -0.3125 to 0.3125
- norm_gain: float32 [2048], P('head'), may hold values from 0.1 to 1.9
- expert_ids: int32 [4096, 6], P('ctx'), may hold values from 0 to 63, all different within a row; in each aligned block of 128 rows (0 to 127, 128 to 255, ...) at most 16 rows name the same one
- combine_weights: float32 [4096, 6], P('ctx'), may hold values from 0.2 to 1
- gate_weight: bfloat16 [64, 1408, 2048], P('ctx', 'head'), may hold values from -0.125 to 0.125
- up_weight: bfloat16 [64, 1408, 2048], P('ctx', 'head'), may hold values from -0.125 to 0.125
- down_weight: bfloat16 [64, 1408, 2048], P('ctx', 'head'), may hold values from -0.15625 to 0.15625
- cotangent: bfloat16 [4096, 2048], P('ctx', 'head'), may hold values from -13 to 13
Outputs:
- moe_output: bfloat16 [4096, 2048], P('ctx', 'head')
- attention_grad: bfloat16 [4096, 2048], P('ctx', 'head')
- residual_grad: bfloat16 [4096, 2048], P('ctx', 'head')
- gain_grad: float32 [2048], P('head')
- combine_grad: float32 [4096, 6], P('ctx')
- gate_grad: bfloat16 [64, 1408, 2048], P('ctx', 'head')
- up_grad: bfloat16 [64, 1408, 2048], P('ctx', 'head')
- down_grad: bfloat16 [64, 1408, 2048], P('ctx', 'head')
Inputs may be any that keep to these rules, and one draw needn't show every extreme that they name: `expert_ids`: each row names 6 different experts. In every aligned block of 128 rows (the rows of one device) no expert is named more than 16 times, and in some blocks one expert is named exactly 16 times.
All inputs are finite; a program needn't handle non-finite values.
Results may differ from a plain program's by a relative error of at most 0.035.
Values may be sent and summed in bfloat16 or wider, within the bound.
A program may use at most 128 MiB of HBM per device.

v0:
```python
import jax
import jax.numpy as jnp
from jax import lax
from jax.sharding import PartitionSpec as P

D = 2048
TOP = 6
EXP_DEV = 2
DH = 128


def attend(query_rows, query_pos, key_rows, value_rows):
    query_count = query_rows.shape[0]
    head_total = query_rows.shape[1] // DH
    query_head_count = query_rows.reshape(query_count, head_total, DH)
    latest = jnp.max(query_pos)
    factor = DH ** (-0.5)
    initial = (
        jnp.full((head_total, query_count), -1e30, jnp.float32),
        jnp.zeros((head_total, query_count), jnp.float32),
        jnp.zeros((head_total, query_count, DH), jnp.float32),
    )
    key_part = lax.all_gather(key_rows, "ctx", axis=0, tiled=True)
    value_part = lax.all_gather(value_rows, "ctx", axis=0, tiled=True)
    key_count = key_part.shape[0]

    def update(current):
        running_max, running_sum, weighted = current
        key_head_count = key_part.reshape(key_count, head_total, DH)
        value_heads = value_part.reshape(key_count, head_total, DH)
        scores = (
            jnp.einsum(
                "sqv,zqv->qsz", query_head_count, key_head_count, preferred_element_type=jnp.float32
            )
            * factor
        )
        key_pos = jnp.arange(key_count, dtype=jnp.int32)
        allowed = query_pos[:, None] >= key_pos[None, :]
        new_max = jnp.maximum(running_max, jnp.max(jnp.where(allowed[None], scores, -1e30), axis=2))
        weights = jnp.where(allowed[None], jnp.exp(scores - new_max[:, :, None]), 0.0)
        running_sum = jnp.sum(weights, axis=2)
        weighted = jnp.einsum(
            "cli,icx->clx",
            weights.astype(jnp.bfloat16),
            value_heads,
            preferred_element_type=jnp.float32,
        )
        return (new_max, running_sum, weighted)

    running_max, running_sum, weighted = lax.cond(
        jnp.int32(0) <= latest, update, lambda current: current, initial
    )
    result = weighted / running_sum[:, :, None]
    return (
        jnp.transpose(result, (1, 0, 2)).reshape(query_count, head_total * DH).astype(jnp.bfloat16)
    )


def place_rows(row_block, factors, targets, total_rows):
    if factors is None:
        spread = jnp.repeat(row_block, TOP, axis=0)
    else:
        spread = (
            (row_block[:, None, :].astype(jnp.float32) * factors[:, :, None])
            .astype(jnp.bfloat16)
            .reshape(-1, row_block.shape[1])
        )
    return jnp.zeros((total_rows, row_block.shape[1]), jnp.bfloat16).at[targets].set(spread)


def deliver(local_rows, factors, targets, expert_count, capacity):
    whole = lax.all_gather(local_rows, "head", axis=1, tiled=True)
    packed = place_rows(whole, factors, targets, expert_count * capacity).reshape(
        expert_count, capacity, whole.shape[1]
    )
    return lax.all_to_all(packed, "ctx", split_axis=0, concat_axis=1, tiled=True)


def collect(partial_value, targets, token_count):
    summed = lax.psum_scatter(
        partial_value.astype(jnp.bfloat16), "head", scatter_dimension=2, tiled=True
    )
    returned = lax.all_to_all(summed, "ctx", split_axis=1, concat_axis=0, tiled=True)
    flat_rows = returned.reshape(-1, returned.shape[2])
    return flat_rows[targets].reshape(token_count, TOP, returned.shape[2])


def per_device(
    queries,
    key_rows,
    value_rows,
    output_weight,
    residual_stream,
    norm_gain,
    expert_ids,
    combine_weights,
    gate_weight,
    up_weight,
    down_weight,
    cotangent,
):
    token_count = queries.shape[0]
    cycle_size = lax.axis_size("ctx")
    expert_count = EXP_DEV * cycle_size
    capacity = max(2, 4 * token_count * TOP // (3 * expert_count))
    device_index = lax.axis_index("ctx")
    positions = device_index * token_count + jnp.arange(token_count, dtype=jnp.int32)
    attention = attend(queries, positions, key_rows, value_rows)
    projection_terms = jnp.dot(attention, output_weight, preferred_element_type=jnp.float32)
    projected = lax.psum_scatter(
        projection_terms.astype(jnp.bfloat16), "head", scatter_dimension=1, tiled=True
    ).astype(jnp.float32)
    hidden_width = residual_stream.astype(jnp.float32) + projected
    squares = lax.psum(jnp.sum(hidden_width * hidden_width, axis=1), "head")
    inverse = lax.rsqrt(squares / D + 1e-06)
    normed = hidden_width * inverse[:, None]
    inputs = (normed * norm_gain).astype(jnp.bfloat16)
    flat_ids = expert_ids.reshape(-1)
    onehot = (flat_ids[:, None] == jnp.arange(expert_count, dtype=jnp.int32)[None, :]).astype(
        jnp.int32
    )
    earlier = jnp.cumsum(onehot, axis=0) - onehot
    slot_index = jnp.sum(earlier * onehot, axis=1)
    targets = flat_ids * capacity + slot_index
    expert_rows = deliver(inputs, None, targets, expert_count, capacity)
    gate_pre = jnp.einsum(
        "erd,efd->erf", expert_rows, gate_weight, preferred_element_type=jnp.float32
    )
    up_pre = jnp.einsum("erd,efd->erf", expert_rows, up_weight, preferred_element_type=jnp.float32)
    sigmoid_gate = jax.nn.sigmoid(gate_pre)
    activation = (gate_pre * sigmoid_gate * up_pre).astype(jnp.bfloat16)
    partial_value = jnp.einsum(
        "erf,efd->erd", activation, down_weight, preferred_element_type=jnp.float32
    )
    picked = collect(partial_value, targets, token_count)
    picked_float = picked.astype(jnp.float32)
    moe_output = jnp.sum(combine_weights[:, :, None] * picked_float, axis=1).astype(jnp.bfloat16)
    pick_terms = jnp.sum(cotangent.astype(jnp.float32)[:, None, :] * picked_float, axis=2)
    combine_grad = lax.psum(pick_terms, "head")
    grad_rows = deliver(cotangent, combine_weights, targets, expert_count, capacity)
    act_grad = jnp.einsum(
        "erd,efd->erf", grad_rows, down_weight, preferred_element_type=jnp.float32
    )
    down_grad = jnp.einsum(
        "erf,erd->efd", activation, grad_rows, preferred_element_type=jnp.float32
    ).astype(jnp.bfloat16)
    gate_delta = (
        act_grad * up_pre * sigmoid_gate * (1.0 + gate_pre * (1.0 - sigmoid_gate))
    ).astype(jnp.bfloat16)
    up_delta = (act_grad * gate_pre * sigmoid_gate).astype(jnp.bfloat16)
    gate_grad = jnp.einsum(
        "erf,erd->efd", gate_delta, expert_rows, preferred_element_type=jnp.float32
    ).astype(jnp.bfloat16)
    up_grad = jnp.einsum(
        "erf,erd->efd", up_delta, expert_rows, preferred_element_type=jnp.float32
    ).astype(jnp.bfloat16)
    row_terms = jnp.einsum(
        "erf,efd->erd", gate_delta, gate_weight, preferred_element_type=jnp.float32
    )
    row_terms = row_terms + jnp.einsum(
        "erf,efd->erd", up_delta, up_weight, preferred_element_type=jnp.float32
    )
    input_grad = jnp.sum(collect(row_terms, targets, token_count).astype(jnp.float32), axis=1)
    gain_grad = lax.psum(jnp.sum(input_grad * normed, axis=0), "ctx")
    normed_grad = input_grad * norm_gain
    centre = lax.psum(jnp.sum(normed_grad * normed, axis=1), "head") / D
    residual_grad = (inverse[:, None] * (normed_grad - normed * centre[:, None])).astype(
        jnp.bfloat16
    )
    attention_grad = jnp.dot(
        lax.all_gather(residual_grad, "head", axis=1, tiled=True),
        output_weight.T,
        preferred_element_type=jnp.float32,
    ).astype(jnp.bfloat16)
    return (
        moe_output,
        attention_grad,
        residual_grad,
        gain_grad,
        combine_grad,
        gate_grad,
        up_grad,
        down_grad,
    )


def solution(mesh):
    return jax.shard_map(
        per_device,
        mesh=mesh,
        in_specs=(
            P("ctx", "head"),
            P("ctx", "head"),
            P("ctx", "head"),
            P("head", None),
            P("ctx", "head"),
            P("head"),
            P("ctx", None),
            P("ctx", None),
            P("ctx", "head", None),
            P("ctx", "head", None),
            P("ctx", "head", None),
            P("ctx", "head"),
        ),
        out_specs=(
            P("ctx", "head"),
            P("ctx", "head"),
            P("ctx", "head"),
            P("head"),
            P("ctx", None),
            P("ctx", "head", None),
            P("ctx", "head", None),
            P("ctx", "head", None),
        ),
        check_vma=False,
    )
```

profile of v0, /device:TPU:2, one launch (start us, length us, event | category | flops | bytes accessed | tf_op | source)
XLA Modules:
  0.0 721.4 jit_solution(1111953436902752528)
XLA Ops:
  11.4 1.8 reduce-window.6
  13.5 29.4 %all_gather.18 = bf16[128,2048]{1,0:T(8,128)(2,1)S(1)} all-gather(bf16[128,256]{1,0:T(8,128)(2,1)} %param.25), channel_id=1, replica_groups=mesh['ctx'=32,'head'=8] {'head'}, dimensions={1}, use_global_device_ids=true | all-gather | bytes 589824 | tf_op jit(solution)/shard_map/all_gather | solution.py:72
  42.9 4.3 mul.146
  47.2 8.3 %mul.147 = f32[768,2048]{1,0:T(8,128)} reshape(f32[128,6,2048]{2,1,0:T(8,128)} %mul.146) | data formatting | bytes 12582912 | tf_op jit(solution)/shard_map/mul | solution.py:64
  55.6 14.4 %scatter_custom_fusion.1 = bf16[1024,2048]{1,0:T(8,128)(2,1)} fusion(s32[768]{0:T(1024)S(1)} %fusion.24, f32[768,2048]{1,0:T(8,128)} %mul.147, f32[768]{0:T(1024)S(1)} %mul.148, bf16[]{:T(256)} %constant.10.clone.1), kind=kCustom, calls=%fused_computation.25 | custom fusion | flops 3145728 | bytes 10489858 | tf_op jit(solution)/shard_map/scatter | solution.py:68
  70.0 10.4 %all-to-all-start.2 = ((bf16[64,16,2048]{2,1,0:T(8,128)(2,1)}), bf16[64,16,2048]{2,1,0:T(8,128)(2,1)}, u32[]{:S(2)}, u32[]{:S(2)}) async-start(bf16[64,16,2048]{2,1,0:T(8,128)(2,1)} %bitcast.96), calls=%async_computation.4 | async-start | bytes 8388608 | tf_op jit(solution)/shard_map/all_to_all | solution.py:76
  82.6 18.6 %all-gather.3.cloned.1.call-done = bf16[4096,256]{1,0:T(8,128)(2,1)} async-done(((bf16[128,256]{1,0:T(8,128)(2,1)}), bf16[4096,256]{1,0:T(8,128)(2,1)}) %all-gather.3.cloned.1.call-update) | async-done | bytes 2097168 | tf_op jit(solution)/shard_map/all_gather | solution.py:23
  101.2 95.9 %all-gather.5.cloned.1.call-done = bf16[4096,256]{1,0:T(8,128)(2,1)} async-done(((bf16[128,256]{1,0:T(8,128)(2,1)}), bf16[4096,256]{1,0:T(8,128)(2,1)}) %all-gather.5.cloned.1.call-update) | async-done | bytes 2097168 | tf_op jit(solution)/shard_map/all_gather | solution.py:24
  197.1 6.4 conditional.1
  198.0 3.0 select_reduce_fusion
  201.0 1.5 fusion.2
  203.6 1.1 convolution_convert_fusion.4
  204.7 38.3 %reduce-scatter.4.cloned.1.call-done = bf16[128,256]{1,0:T(8,128)(2,1)} async-done(((bf16[128,2048]{1,0:T(8,128)(2,1)}), bf16[128,256]{1,0:T(8,128)(2,1)}) %reduce-scatter.4.cloned.1.call-update) | async-done | bytes 65552 | tf_op jit(solution)/shard_map/reduce_scatter | solution.py:110
  243.9 17.5 %psum.28 = f32[128]{0:T(128)S(1)} all-reduce(f32[128]{0:T(128)S(1)} %multiply_reduce_fusion.4), channel_id=1, replica_groups=mesh['ctx'=32,'head'=8] {'head'}, use_global_device_ids=true, to_apply=%region_10.11 | all-reduce | flops 128 | bytes 1024 | tf_op jit(solution)/shard_map/psum | solution.py:114
  262.3 29.1 %all_gather.17 = bf16[128,2048]{1,0:T(8,128)(2,1)S(1)} all-gather(bf16[128,256]{1,0:T(8,128)(2,1)S(1)} %multiply_convert_fusion.6), channel_id=1, replica_groups=mesh['ctx'=32,'head'=8] {'head'}, dimensions={1}, use_global_device_ids=true | all-gather | bytes 589824 | tf_op jit(solution)/shard_map/all_gather | solution.py:72
  291.4 2.6 broadcast_in_dim.34
  294.1 6.3 reshape.167
  300.4 10.4 %scatter_custom_fusion = bf16[1024,2048]{1,0:T(8,128)(2,1)} fusion(s32[768]{0:T(1024)S(1)} %fusion.24, bf16[768,2048]{1,0:T(8,128)(2,1)} %reshape.167, bf16[]{:T(256)} %constant.10.clone.1), kind=kCustom, calls=%fused_computation.32 | custom fusion | bytes 4194816 | tf_op jit(solution)/shard_map/scatter | solution.py:68
  310.8 8.9 %all-to-all-start = ((bf16[64,16,2048]{2,1,0:T(8,128)(2,1)}), bf16[64,16,2048]{2,1,0:T(8,128)(2,1)}, u32[]{:S(2)}, u32[]{:S(2)}) async-start(bf16[64,16,2048]{2,1,0:T(8,128)(2,1)} %bitcast.99), calls=%async_computation.1 | async-start | bytes 8388608 | tf_op jit(solution)/shard_map/all_to_all | solution.py:76
  319.9 4.7 copy.54
  324.6 91.9 %all-to-all-done = bf16[64,16,2048]{2,1,0:T(8,128)(2,1)} async-done(((bf16[64,16,2048]{2,1,0:T(8,128)(2,1)}), bf16[64,16,2048]{2,1,0:T(8,128)(2,1)}, u32[]{:S(2)}, u32[]{:S(2)}) %all-to-all-start) | async-done | bytes 4194336 | tf_op jit(solution)/shard_map/all_to_all | solution.py:76
  416.5 2.6 copy.50
  419.2 1.5 fusion.27
  421.6 1.6 fusion.26
  423.8 1.8 multiply_convert_fusion.2
  426.3 3.3 convolution_convert_fusion
  429.6 2.8 fusion.28
  432.4 3.3 add_convert_fusion
  435.8 45.7 %reduce-scatter.6.cloned.1.call-done = bf16[2,512,256]{2,1,0:T(8,128)(2,1)} async-done(((bf16[2,512,2048]{2,1,0:T(8,128)(2,1)}), bf16[2,512,256]{2,1,0:T(8,128)(2,1)}) %reduce-scatter.6.cloned.1.call-update) | async-done | bytes 524304 | tf_op jit(solution)/shard_map/reduce_scatter | solution.py:80
  481.5 2.4 copy.51
  483.8 9.2 %all-to-all-start.1 = ((bf16[2,512,256]{2,0,1:T(2,128)(2,1)}), bf16[2,512,256]{2,0,1:T(2,128)(2,1)S(1)}, u32[]{:S(2)}, u32[]{:S(2)}) async-start(bf16[2,512,256]{2,0,1:T(2,128)(2,1)} %copy.51), calls=%async_computation.3 | async-start | bytes 1048576 | tf_op jit(solution)/shard_map/all_to_all | solution.py:83
  493.7 49.6 %reduce-scatter.8.cloned.1.call-done = bf16[2,512,256]{2,1,0:T(8,128)(2,1)} async-done(((bf16[2,512,2048]{2,1,0:T(8,128)(2,1)}), bf16[2,512,256]{2,1,0:T(8,128)(2,1)}) %reduce-scatter.8.cloned.1.call-update) | async-done | bytes 524304 | tf_op jit(solution)/shard_map/reduce_scatter | solution.py:80
  543.3 2.4 copy.55
  545.8 8.8 %all-to-all-start.3 = ((bf16[2,512,256]{2,0,1:T(2,128)(2,1)}), bf16[2,512,256]{2,0,1:T(2,128)(2,1)}, u32[]{:S(2)}, u32[]{:S(2)}) async-start(bf16[2,512,256]{2,0,1:T(2,128)(2,1)} %copy.55), calls=%async_computation.6 | async-start | bytes 1048576 | tf_op jit(solution)/shard_map/all_to_all | solution.py:83
  554.6 4.5 convolution_convert_fusion.1
  559.0 2.0 convolution_convert_fusion.2
  561.1 2.0 convolution_convert_fusion.3
  563.2 2.7 gather_fusion
  567.0 7.6 %all-to-all-done.3 = bf16[2,512,256]{2,0,1:T(2,128)(2,1)} async-done(((bf16[2,512,256]{2,0,1:T(2,128)(2,1)}), bf16[2,512,256]{2,0,1:T(2,128)(2,1)}, u32[]{:S(2)}, u32[]{:S(2)}) %all-to-all-start.3) | async-done | bytes 524320 | tf_op jit(solution)/shard_map/all_to_all | solution.py:83
  574.5 1.1 copy.56
  575.7 2.7 gather_fusion.1
  578.3 1.1 reshape.146
  579.5 1.5 reduce_sum.78
  581.2 65.6 %psum.30 = f32[256]{0:T(256)} all-reduce(f32[256]{0:T(256)S(1)} %get-tuple-element.38), channel_id=1, replica_groups=mesh['ctx'=32,'head'=8] {'ctx'}, use_global_device_ids=true, to_apply=%region_20.21 | all-reduce | flops 256 | bytes 2048 | tf_op jit(solution)/shard_map/psum | solution.py:164
  646.8 2.6 multiply_reduce_fusion
  649.3 34.5 %all-reduce = (f32[128]{0:T(128)S(1)}, f32[128,6]{1,0:T(8,128)S(1)}) all-reduce(f32[128]{0:T(128)S(1)} %get-tuple-element.39, f32[128,6]{1,0:T(8,128)S(1)} %get-tuple-element.36), channel_id=1, replica_groups=mesh['ctx'=32,'head'=8] {'head'}, use_global_device_ids=true, to_apply=%region_18.19 | all-reduce | flops 896 | bytes 7168 | tf_op jit(solution)/shard_map/psum | solution.py:166
  684.6 28.8 %all_gather.19 = bf16[128,2048]{1,0:T(8,128)(2,1)S(1)} all-gather(bf16[128,256]{1,0:T(8,128)(2,1)S(1)} %multiply_convert_fusion.5), channel_id=1, replica_groups=mesh['ctx'=32,'head'=8] {'head'}, dimensions={1}, use_global_device_ids=true | all-gather | bytes 589824 | tf_op jit(solution)/shard_map/all_gather | solution.py:171
  713.5 1.1 convolution_convert_fusion.5
  (82 shorter events, 14.7 us)
Async XLA Ops:
  7.2 416.0 %copy-start = (bf16[2,176,2048]{2,1,0:T(8,128)(2,1)S(1)}, bf16[2,176,2048]{2,1,0:T(8,128)(2,1)}, u32[]{:S(2)}) copy-start(bf16[2,176,2048]{2,1,0:T(8,128)(2,1)} %param.24) | copy-start | bytes 4325380
  7.2 94.0 %all-gather.3.cloned.1.call-start = ((), (), s32[]{:S(2)}) async-start(), calls=%async_computation.7 | async-start | bytes 2162688 | tf_op jit(solution)/shard_map/all_gather | solution.py:23
  10.7 0.6 copy-start.14
  70.0 127.1 %copy-start.19 = (bf16[128,256]{1,0:T(8,128)(2,1)S(1)}, bf16[128,256]{1,0:T(8,128)(2,1)}, u32[]{:S(2)}) copy-start(bf16[128,256]{1,0:T(8,128)(2,1)} %param.14) | copy-start | bytes 196612
  70.0 240.8 %all-to-all-start.2 = ((bf16[64,16,2048]{2,1,0:T(8,128)(2,1)}), bf16[64,16,2048]{2,1,0:T(8,128)(2,1)}, u32[]{:S(2)}, u32[]{:S(2)}) async-start(bf16[64,16,2048]{2,1,0:T(8,128)(2,1)} %bitcast.96), calls=%async_computation.4 | async-start | bytes 8388608 | tf_op jit(solution)/shard_map/all_to_all | solution.py:76
  80.5 116.6 %all-gather.5.cloned.1.call-start = ((), (), s32[]{:S(2)}) async-start(), calls=%async_computation.8 | async-start | bytes 2162688 | tf_op jit(solution)/shard_map/all_gather | solution.py:24
  81.2 161.8 %reduce-scatter.4.cloned.1.call-start = ((), (), s32[]{:S(2)}) async-start(), calls=%async_computation.9 | async-start | bytes 589824 | tf_op jit(solution)/shard_map/reduce_scatter | solution.py:110
  197.1 6.5 copy-start.4
  197.1 45.9 %copy-start.11 = (bf16[128,256]{1,0:T(8,128)(2,1)S(1)}, bf16[128,256]{1,0:T(8,128)(2,1)}, u32[]{:S(2)}) copy-start(bf16[128,256]{1,0:T(8,128)(2,1)} %param.18) | copy-start | bytes 196612
  197.1 64.3 %copy-start.17 = (f32[256]{0:T(256)S(1)}, f32[256]{0:T(256)}, u32[]{:S(2)}) copy-start(f32[256]{0:T(256)} %param.19) | copy-start | bytes 3076
  197.6 3.4 copy-start.18
  310.8 105.7 %all-to-all-start = ((bf16[64,16,2048]{2,1,0:T(8,128)(2,1)}), bf16[64,16,2048]{2,1,0:T(8,128)(2,1)}, u32[]{:S(2)}, u32[]{:S(2)}) async-start(bf16[64,16,2048]{2,1,0:T(8,128)(2,1)} %bitcast.99), calls=%async_computation.1 | async-start | bytes 8388608 | tf_op jit(solution)/shard_map/all_to_all | solution.py:76
  319.7 161.8 %reduce-scatter.6.cloned.1.call-start = ((), (), s32[]{:S(2)}) async-start(), calls=%async_computation.10 | async-start | bytes 4718592 | tf_op jit(solution)/shard_map/reduce_scatter | solution.py:80
  416.5 2.6 copy-start.6
  419.1 4.0 copy-start.1
  419.1 2.4 copy-start.5
  421.6 2.2 copy-start.3
  425.5 0.7 copy-start.10
  425.5 4.1 copy-start.8
  429.6 113.8 %reduce-scatter.8.cloned.1.call-start = ((), (), s32[]{:S(2)}) async-start(), calls=%async_computation.11 | async-start | bytes 4718592 | tf_op jit(solution)/shard_map/reduce_scatter | solution.py:80
  429.6 2.8 copy-start.7
  435.8 57.3 %copy-start.15 = (bf16[128,256]{1,0:T(8,128)(2,1)S(1)}, bf16[128,256]{1,0:T(8,128)(2,1)}, u32[]{:S(2)}) copy-start(bf16[128,256]{1,0:T(8,128)(2,1)} %param.25) | copy-start | bytes 196612
  483.8 61.9 %all-to-all-start.1 = ((bf16[2,512,256]{2,0,1:T(2,128)(2,1)}), bf16[2,512,256]{2,0,1:T(2,128)(2,1)S(1)}, u32[]{:S(2)}, u32[]{:S(2)}) async-start(bf16[2,512,256]{2,0,1:T(2,128)(2,1)} %copy.51), calls=%async_computation.3 | async-start | bytes 1048576 | tf_op jit(solution)/shard_map/all_to_all | solution.py:83
  545.8 28.8 %all-to-all-start.3 = ((bf16[2,512,256]{2,0,1:T(2,128)(2,1)}), bf16[2,512,256]{2,0,1:T(2,128)(2,1)}, u32[]{:S(2)}, u32[]{:S(2)}) async-start(bf16[2,512,256]{2,0,1:T(2,128)(2,1)} %copy.55), calls=%async_computation.6 | async-start | bytes 1048576 | tf_op jit(solution)/shard_map/all_to_all | solution.py:83
  554.5 4.5 copy-start.2
  559.0 2.0 copy-start.9
  565.8 15.2 %copy-start.12 = (bf16[128,256]{1,0:T(8,128)(2,1)S(1)}, bf16[128,256]{1,0:T(8,128)(2,1)}, u32[]{:S(2)}) copy-start(bf16[128,256]{1,0:T(8,128)(2,1)} %param.18) | copy-start | bytes 196612
  565.9 15.2 %copy-start.13 = (bf16[128,256]{1,0:T(8,128)(2,1)S(1)}, bf16[128,256]{1,0:T(8,128)(2,1)}, u32[]{:S(2)}) copy-start(bf16[128,256]{1,0:T(8,128)(2,1)} %reduce-scatter.4.cloned.1.call-done) | copy-start | bytes 196612
  684.6 30.0 %copy-start.16 = (bf16[128,256]{1,0:T(8,128)(2,1)}, bf16[128,256]{1,0:T(8,128)(2,1)S(1)}, u32[]{:S(2)}) copy-start(bf16[128,256]{1,0:T(8,128)(2,1)S(1)} %multiply_convert_fusion.5) | copy-start | bytes 196612
Sparse Core Ops, SparseCore 0:
  10.8 90.3 all-gather.2
  104.0 93.0 all-gather.4
  204.8 38.0 reduce-scatter.3
  429.7 51.7 reduce-scatter.5
  484.0 59.2 reduce-scatter.7
where the time goes:
time: 730 us; the launch traced here: 721 us
  waiting for transfers between devices  349 us (48%)
  blocking collectives  205 us (28%)
  local copies, waits for them, and re-layouts  58.7 us (8%)
  starting transfers between devices  37.7 us (5%)
  matrix products  29.5 us (4%)
  other arithmetic  26.2 us (4%)
  between operations  15 us (2%)
    all_gather x1, waiting for transfers between devices, attend(): value_part = lax.all_gather(value_rows, 'ctx', axis=0, tiled=True)  95.9 us
    reduce_scatter x2, waiting for transfers between devices, collect(): lax.psum_scatter(partial_value.astype(jnp.bfloat16), 'head', scatter_dime...  95.2 us
    all_to_all x2, waiting for transfers between devices, deliver(): lax.all_to_all(packed, 'ctx', split_axis=0, concat_axis=1, tiled=True)  91.9 us
    psum x1, blocking collectives, per_device(): gain_grad = lax.psum(jnp.sum(input_grad * normed, axis=0), 'ctx')  65.6 us
    all_gather x2, blocking collectives, deliver(): whole = lax.all_gather(local_rows, 'head', axis=1, tiled=True)  58.5 us
    reduce_scatter x1, waiting for transfers between devices, per_device(): lax.psum_scatter(projection_terms.astype(jnp.bfloat16), 'head', scatter_d...  38.3 us
    psum x1, blocking collectives, per_device(): centre = lax.psum(jnp.sum(normed_grad * normed, axis=1), 'head') / D  34.5 us
    all_gather x1, blocking collectives, per_device(): lax.all_gather(residual_grad, 'head', axis=1, tiled=True)  28.8 us
  transfers between devices with their start and end apart: 9, of which 7 were waited for; matrix products, arithmetic and copies ran while one was open for 12% of the time, Pallas kernels for 0%

commit v1 on v0

v1 whole, which is shorter than its diff:
```python
import functools

import jax
import jax.numpy as jnp
from jax import lax
from jax.experimental import pallas as pl
from jax.experimental.pallas import tpu as pltpu
from jax.sharding import PartitionSpec as P

D = 2048
TOP = 6
DH = 128
NC = 32
NH = 8
TOK = 128
W = 256
FD = 176
CAP = 16
ROWS = NC * CAP
SLOTS = 2 * ROWS
MESH = pl.DeviceIdType.MESH
BF = jnp.bfloat16
F32 = jnp.float32


def dot(a, b, ca=1, cb=0):
    return lax.dot_general(a, b, (((ca,), (cb,)), ((), ())), preferred_element_type=F32)


def coords():
    return lax.axis_index("ctx"), lax.axis_index("head")


def head_of(xl, y):
    return xl * 4 + lax.rem(y + 4, 4)


def ctx_of(xh, z, core):
    return xh * 16 + lax.rem(z + 8, 8) * 2 + core


def remote(src, dst, ssem, rsem, ctx, head):
    return pltpu.make_async_remote_copy(
        src, dst, ssem, rsem, device_id=(ctx, head), device_id_type=MESH
    )


def greet():
    i, h = coords()
    bar = pltpu.get_barrier_semaphore()

    def ctx_peer(o, c):
        pl.semaphore_signal(bar, 1, device_id=(lax.rem(i + o, NC), h), device_id_type=MESH)
        return c

    def head_peer(o, c):
        pl.semaphore_signal(bar, 1, device_id=(i, lax.rem(h + o, NH)), device_id_type=MESH)
        return c

    lax.fori_loop(1, NC, ctx_peer, 0)
    lax.fori_loop(1, NH, head_peer, 0)
    pl.semaphore_wait(bar, NC - 1 + NH - 1)


def run_flows(*flows):
    flows = list(flows)
    while flows:
        for f in list(flows):
            try:
                next(f)
            except StopIteration:
                flows.remove(f)


def start_dispatch(packed, g, asend, arecv, lsem):
    i, h = coords()
    mine = pl.ds(pl.multiple_of(i * CAP, CAP), CAP)

    def send(o, c):
        d = lax.rem(i + o, NC)
        theirs = pl.ds(pl.multiple_of(d * CAP, CAP), CAP)
        remote(packed.at[:, theirs], g.at[h, :, mine], asend.at[o], arecv.at[o], d, h).start()
        return c

    own = pltpu.make_async_copy(packed.at[:, mine], g.at[h, :, mine], lsem)
    own.start()
    lax.fori_loop(1, NC, send, 0)
    own.wait()


def wait_dispatch(packed, g, asend, arecv):
    i, h = coords()

    def one(o, c):
        s = lax.rem(i - o + NC, NC)
        theirs = pl.ds(pl.multiple_of(s * CAP, CAP), CAP)
        remote(packed.at[:, theirs], g.at[h, :, theirs], asend.at[o], arecv.at[o], s, h).wait()
        return c

    lax.fori_loop(1, NC, one, 0)


def gather_flow(g, gate, ssem, rsem):
    i, h = coords()
    xl, y = h // 4, lax.rem(h, 4)
    xp, up, down = head_of(1 - xl, y), head_of(xl, y + 1), head_of(xl, y - 1)
    pup, pdown = head_of(1 - xl, y + 1), head_of(1 - xl, y - 1)
    far, pfar = head_of(xl, y + 2), head_of(1 - xl, y + 2)
    half_rows = ROWS // 2
    chunks = [(e, hf) for hf in range(2) for e in range(2)]

    def copy(kind, c, block, target):
        e, hf = c
        view = g.at[block, e, pl.ds(hf * half_rows, half_rows)]
        n = e * 2 + hf
        return remote(view, view, ssem.at[kind, n], rsem.at[kind, n], i, target)

    gate()
    for c in chunks:
        copy(0, c, h, xp).start()
        copy(1, c, h, up).start()
        copy(2, c, h, down).start()
    yield
    for c in chunks:
        copy(0, c, xp, xp).wait_recv()
        copy(3, c, xp, up).start()
        copy(4, c, xp, down).start()
        yield
        if c[0] == 0:
            copy(1, c, down, up).wait_recv()
            copy(5, c, down, up).start()
        else:
            copy(2, c, up, down).wait_recv()
            copy(5, c, up, down).start()
        yield
    for c in chunks:
        copy(5, c, far, up).wait_recv()
        copy(6, c, far, xp).start()
        yield
    for c in chunks:
        if c[0] == 0:
            copy(2, c, up, up).wait_recv()
        else:
            copy(1, c, down, up).wait_recv()
        copy(3, c, pdown, up).wait_recv()
        copy(4, c, pup, up).wait_recv()
        copy(6, c, pfar, up).wait_recv()
        yield
    for c in chunks:
        copy(0, c, h, xp).wait_send()
        copy(1, c, h, up).wait_send()
        copy(2, c, h, down).wait_send()
        copy(3, c, xp, up).wait_send()
        copy(4, c, xp, down).wait_send()
        copy(5, c, down, up).wait_send()
        copy(6, c, far, xp).wait_send()
    yield


def kv_flow(kv, zs, zr, ks, kr, ps, pr):
    i, h = coords()
    xh, z, core = i // 16, lax.rem(i // 2, 8), lax.rem(i, 2)
    other = ctx_of(1 - xh, z, core)
    up, down = ctx_of(xh, z + 1, core), ctx_of(xh, z - 1, core)
    twin = ctx_of(xh, z, 1 - core)

    def cross(block):
        return remote(kv.at[block], kv.at[block], ps, pr, other, h)

    def ring(k, d, s):
        half = xh if k == 0 else 1 - xh
        block = ctx_of(half, z - s if d == 0 else z + s, core)
        return remote(kv.at[block], kv.at[block], zs.at[k, d, s], zr.at[k, d, s], up if d == 0 else down, h)

    def landed(k, d, s):
        half = xh if k == 0 else 1 - xh
        block = ctx_of(half, z - s - 1 if d == 0 else z + s + 1, core)
        return remote(kv.at[block], kv.at[block], zs.at[k, d, s], zr.at[k, d, s], up if d == 0 else down, h)

    def share(half, dz):
        block = ctx_of(half, z + dz, core)
        n = (0 if half is xh else 8) + dz % 8
        return remote(kv.at[block], kv.at[block], ks.at[n], kr.at[n], twin, h)

    def shared(half, dz):
        block = ctx_of(half, z + dz, 1 - core)
        n = (0 if half is xh else 8) + dz % 8
        return remote(kv.at[block], kv.at[block], ks.at[n], kr.at[n], twin, h)

    halves = (xh, 1 - xh)
    cross(i).start()
    ring(0, 0, 0).start()
    ring(0, 1, 0).start()
    share(halves[0], 0).start()
    yield
    cross(other).wait_recv()
    ring(1, 0, 0).start()
    ring(1, 1, 0).start()
    share(halves[1], 0).start()
    yield
    for s in range(4):
        for k in range(2):
            landed(k, 0, s).wait_recv()
            if s < 3:
                ring(k, 0, s + 1).start()
            share(halves[k], -s - 1).start()
            if s < 3:
                landed(k, 1, s).wait_recv()
                if s < 2:
                    ring(k, 1, s + 1).start()
                share(halves[k], s + 1).start()
            yield
    cross(i).wait_send()
    for k in range(2):
        for s in range(4):
            ring(k, 0, s).wait_send()
        for s in range(3):
            ring(k, 1, s).wait_send()
        for dz in range(-4, 4):
            share(halves[k], dz).wait_send()
            shared(halves[k], dz).wait_recv()
    yield


def routing(ids, cw):
    eio = lax.broadcasted_iota(jnp.int32, (TOK, 2 * NC), 1)
    hot = jnp.zeros((TOK, 2 * NC), F32)
    wts = jnp.zeros((TOK, 2 * NC), F32)
    for k in range(TOP):
        m = ids[:, k : k + 1] == eio
        hot = hot + jnp.where(m, 1.0, 0.0)
        wts = wts + jnp.where(m, cw[:, k : k + 1], 0.0)
    r = lax.broadcasted_iota(jnp.int32, (TOK, TOK), 0)
    c = lax.broadcasted_iota(jnp.int32, (TOK, TOK), 1)
    lower = jnp.where(c < r, 1.0, 0.0).astype(BF)
    earlier = dot(lower, hot.astype(BF))
    n = lax.broadcasted_iota(jnp.int32, (2 * NC, SLOTS), 1)
    e = lax.broadcasted_iota(jnp.int32, (2 * NC, SLOTS), 0)
    spread = jnp.where(e == 2 * (lax.rem(n, ROWS) // CAP) + n // ROWS, 1.0, 0.0).astype(BF)
    hot_n = dot(hot.astype(BF), spread)
    earlier_n = dot(earlier.astype(BF), spread)
    slot = lax.rem(lax.broadcasted_iota(jnp.int32, (TOK, SLOTS), 1), CAP).astype(F32)
    place = jnp.where((hot_n > 0.5) & (earlier_n == slot), 1.0, 0.0)
    hi = wts.astype(BF)
    lo = (wts - hi.astype(F32)).astype(BF)
    whi = place * dot(hi, spread)
    wlo = place * dot(lo, spread)
    return place.astype(BF), whi.astype(BF), wlo.astype(BF)


def kernel_a(k_ref, v_ref, ids_ref, cw_ref, cot_ref, kv, g, place, whi, wlo,
             packed, lsem, zs, zr, ks, kr, ps, pr, asend, arecv, gs, gr):
    i, h = coords()
    greet()
    a = pltpu.make_async_copy(k_ref, kv.at[i, 0], lsem.at[0])
    b = pltpu.make_async_copy(v_ref, kv.at[i, 1], lsem.at[1])
    a.start()
    b.start()
    a.wait()
    b.wait()
    flow = kv_flow(kv, zs, zr, ks, kr, ps, pr)
    next(flow)
    p, hi, lo = routing(ids_ref[...], cw_ref[...])
    place[...] = p
    whi[...] = hi
    wlo[...] = lo
    cot = cot_ref[...]
    rows = dot(hi, cot, 0, 0) + dot(lo, cot, 0, 0)
    packed[...] = rows.astype(BF).reshape(2, ROWS, W)
    start_dispatch(packed, g, asend, arecv, lsem.at[2])
    next(flow)
    run_flows(gather_flow(g, lambda: wait_dispatch(packed, g, asend, arecv), gs, gr), flow)


def exchange_stats(buf, ssem, rsem):
    i, h = coords()
    for o in range(1, NH):
        d = lax.rem(h + o, NH)
        remote(buf.at[0], buf.at[o], ssem.at[o], rsem.at[o], i, d).start()
    total = buf[0]
    for o in range(1, NH):
        d = lax.rem(h + o, NH)
        remote(buf.at[0], buf.at[o], ssem.at[o], rsem.at[o], i, d).wait()
        total = total + buf[o]
    return total


def kernel_b(att, w_ref, res, gain, place, g, normed, inv,
             terms, got, stats, packed, lsem, ts, tr, ss, sr, asend, arecv, gs, gr):
    i, h = coords()
    greet()
    t = dot(att[...], w_ref[...]).astype(BF)
    for d in range(NH):
        terms[d] = t[:, d * W : (d + 1) * W]
    for o in range(1, NH):
        d = lax.rem(h + o, NH)
        remote(terms.at[d], got.at[o], ts.at[o], tr.at[o], i, d).start()
    hidden = terms[h].astype(F32)
    for o in range(1, NH):
        d = lax.rem(h + o, NH)
        remote(terms.at[d], got.at[o], ts.at[o], tr.at[o], i, d).wait()
        hidden = hidden + got[o].astype(F32)
    hidden = hidden + res[...].astype(F32)
    squares = jnp.sum(hidden * hidden, axis=1, keepdims=True)
    stats[0] = jnp.broadcast_to(squares, (TOK, TOK)).T[0:8]
    total = exchange_stats(stats, ss, sr)
    total = jnp.broadcast_to(total[0:1], (TOK, TOK)).T
    inverse = lax.rsqrt(total / D + 1e-06)
    inv[...] = inverse
    nrm = hidden * inverse[:, 0:1]
    normed[...] = nrm
    inputs = (nrm * gain[...]).astype(BF)
    packed[...] = dot(place[...], inputs, 0, 0).astype(BF).reshape(2, ROWS, W)
    start_dispatch(packed, g, asend, arecv, lsem)
    run_flows(gather_flow(g, lambda: wait_dispatch(packed, g, asend, arecv), gs, gr))


def kernel_c(gin, gcot, wg, wu, wd, ids_ref, place, whi, wlo, cot_ref, normed, inv, gain, w_ref,
             moe, attg, resg, gaing, combg, dgate, dup, ddown,
             act_s, gd_s, ud_s, gp_s, up_s, t_ref, r_ref, fin, picked, stats, rgb, gsum,
             lsem, fs, fr, bs, br, ss, sr, rs, rr, qs, qr):
    i, h = coords()
    xl, y = h // 4, lax.rem(h, 4)
    xp, up, down = head_of(1 - xl, y), head_of(xl, y + 1), head_of(xl, y - 1)
    pup, pdown = head_of(1 - xl, y + 1), head_of(1 - xl, y - 1)
    far, pfar = head_of(xl, y + 2), head_of(1 - xl, y + 2)
    HR = ROWS // 2
    greet()

    def rows_of(ref, e, lo, n):
        return jnp.concatenate([ref[b, e, lo : lo + n] for b in range(NH)], axis=1)

    def forward(e, hf):
        sl = slice(hf * HR, (hf + 1) * HR)
        x = rows_of(gin, e, hf * HR, HR)
        gp = dot(x, wg[e], 1, 1)
        u = dot(x, wu[e], 1, 1)
        gp_s[e, sl] = gp
        up_s[e, sl] = u
        act = (gp * jax.nn.sigmoid(gp) * u).astype(BF)
        act_s[e, sl] = act
        for b in range(NH):
            t_ref[0, b, e, sl] = dot(act, wd[e, :, b * W : (b + 1) * W]).astype(BF)

    def backward(e, hf):
        sl = slice(hf * HR, (hf + 1) * HR)
        x = rows_of(gcot, e, hf * HR, HR)
        ag = dot(x, wd[e], 1, 1)
        gp = gp_s[e, sl]
        s = jax.nn.sigmoid(gp)
        gd = (ag * up_s[e, sl] * s * (1.0 + gp * (1.0 - s))).astype(BF)
        ud = (ag * gp * s).astype(BF)
        gd_s[e, sl] = gd
        ud_s[e, sl] = ud
        for b in range(NH):
            cs = slice(b * W, (b + 1) * W)
            t_ref[1, b, e, sl] = (dot(gd, wg[e, :, cs]) + dot(ud, wu[e, :, cs])).astype(BF)

    def weight_grads(e):
        for b in range(NH):
            cs = slice(b * W, (b + 1) * W)
            x = gin[b, e]
            dgate[e, :, cs] = dot(gd_s[e], x, 0, 0).astype(BF)
            dup[e, :, cs] = dot(ud_s[e], x, 0, 0).astype(BF)
            ddown[e, :, cs] = dot(act_s[e], gcot[b, e], 0, 0).astype(BF)

    def tview(f, block):
        t, e, hf = f
        return t_ref.at[t, block, e, pl.ds(hf * HR, HR)]

    def copy(kind, f, block, target):
        n = f[0] * 4 + f[1] * 2 + f[2]
        return remote(tview(f, block), r_ref.at[n, kind], fs.at[kind, n], fr.at[kind, n], i, target)

    def add(f, block, kinds):
        n = f[0] * 4 + f[1] * 2 + f[2]
        v = tview(f, block)
        acc = v[...].astype(F32)
        for kind in kinds:
            acc = acc + r_ref[n, kind].astype(F32)
        return acc.astype(BF)

    def stage0(f):
        copy(0, f, pfar, xp).start()
        copy(1, f, pup, up).start()
        copy(2, f, pdown, down).start()
        if f[2] == 0:
            copy(6, f, down, down).start()
        else:
            copy(5, f, up, up).start()

    def stage1(f):
        copy(0, f, far, xp).wait_recv()
        tview(f, far)[...] = add(f, far, (0,))
        copy(3, f, far, up if f[2] == 0 else down).start()
        copy(1, f, xp, up).wait_recv()
        copy(2, f, xp, up).wait_recv()
        tview(f, xp)[...] = add(f, xp, (1, 2))
        copy(4, f, xp, xp).start()

    def stage2(f):
        block = up if f[2] == 0 else down
        copy(3, f, block, up).wait_recv()
        tview(f, block)[...] = add(f, block, (3,))
        copy(5 if f[2] == 0 else 6, f, block, block).start()

    def stage3(f):
        t, e, hf = f
        for kind in (4, 5, 6):
            copy(kind, f, h, up).wait_recv()
        fin[t, e, hf * HR : (hf + 1) * HR] = add(f, h, (4, 5, 6))

        def send(k, c):
            d = hf * 16 + k

            @pl.when(d != i)
            def _():
                back(t, e, d).start()

            return c

        lax.fori_loop(0, 16, send, 0)

    def back(t, e, d):
        return remote(fin.at[t, e, pl.ds(pl.multiple_of(d * CAP, CAP), CAP)], picked.at[t, e, i],
                      bs.at[t, e], br.at[t, e], d, h)

    def drain(f):
        for kind, block in ((0, pfar), (1, pup), (2, pdown), (3, far), (4, xp), (5, up), (6, down)):
            copy(kind, f, block, xp).wait_send()

    flows = [(t, e, hf) for t in range(2) for e in range(2) for hf in range(2)]
    for n in range(len(flows) + 3):
        if n < len(flows):
            t, e, hf = flows[n]
            (forward if t == 0 else backward)(e, hf)
            stage0(flows[n])
        elif n == len(flows):
            weight_grads(0)
        elif n == len(flows) + 1:
            weight_grads(1)
        if 0 <= n - 1 < len(flows):
            stage1(flows[n - 1])
        if 0 <= n - 2 < len(flows):
            stage2(flows[n - 2])
        if 0 <= n - 3 < len(flows):
            stage3(flows[n - 3])

    def landed(t):
        mine = pl.ds(pl.multiple_of(i * CAP, CAP), CAP)
        for e in range(2):
            own = pltpu.make_async_copy(fin.at[t, e, mine], picked.at[t, e, i], lsem)
            own.start()
            own.wait()
            part = picked.at[t, e, pl.ds(0, NC - 1)]
            remote(part, part, bs.at[t, e], br.at[t, e], i, xp).wait()
        return picked[t].reshape(SLOTS, W)

    rows = landed(0)
    hi, lo = whi[...], wlo[...]
    moe[...] = (dot(hi, rows) + dot(lo, rows)).astype(BF)
    every = dot(cot_ref[...], rows, 1, 1)
    pl_f = place[...].astype(F32)
    every = every * pl_f
    n = lax.broadcasted_iota(jnp.int32, (TOK, SLOTS), 1)
    expert = 2 * (lax.rem(n, ROWS) // CAP) + n // ROWS
    ids = ids_ref[...]
    lane = lax.broadcasted_iota(jnp.int32, (TOK, TOK), 1)
    packed = jnp.zeros((TOK, TOK), F32)
    for k in range(TOP):
        term = jnp.sum(jnp.where(expert == ids[:, k : k + 1], every, 0.0), axis=1, keepdims=True)
        packed = jnp.where(lane == k, term, packed)

    rows = landed(1)
    input_grad = dot(place[...], rows)
    nrm = normed[...]
    gsum[0] = jnp.broadcast_to(jnp.sum(input_grad * nrm, axis=0, keepdims=True), (8, W))

    def gain_copy(o):
        d = lax.rem(i + o, NC)
        return remote(gsum.at[0], gsum.at[o], qs.at[o], qr.at[o], d, h)

    def gain_start(o, c):
        gain_copy(o).start()
        return c

    ng = input_grad * gain[...]
    packed = jnp.where(lane == TOP, jnp.sum(ng * nrm, axis=1, keepdims=True), packed)
    stats[0] = packed.T[0:8]
    total = exchange_stats(stats, ss, sr)
    lax.fori_loop(1, NC, gain_start, 0)
    total = jnp.concatenate([total, jnp.zeros((TOK - 8, TOK), F32)], axis=0).T
    combg[...] = total[:, 0:TOP]
    centre = total[:, TOP : TOP + 1] / D
    rg = (inv[:, 0:1] * (ng - nrm * centre)).astype(BF)
    resg[...] = rg
    rgb[h] = rg
    for o in range(1, NH):
        d = lax.rem(h + o, NH)
        remote(rgb.at[h], rgb.at[h], rs.at[o], rr.at[o], i, d).start()
    for o in range(1, NH):
        s = lax.rem(h - o + NH, NH)
        remote(rgb.at[s], rgb.at[s], rs.at[o], rr.at[o], i, s).wait()
    whole = jnp.concatenate([rgb[b] for b in range(NH)], axis=1)
    attg[...] = dot(whole, w_ref[...], 1, 1).astype(BF)

    def gain_wait(o, c):
        gain_copy(o).wait()
        return c + gsum[o]

    gaing[...] = lax.fori_loop(1, NC, gain_wait, gsum[0])
    for f in flows:
        drain(f)


VM = pl.BlockSpec(memory_space=pltpu.VMEM)
ANY = pl.BlockSpec(memory_space=pl.ANY)
DMA = pltpu.SemaphoreType.DMA
SDS = jax.ShapeDtypeStruct


def params(n, mib):
    return pltpu.CompilerParams(collective_id=n, has_side_effects=True, vmem_limit_bytes=mib << 20)


def gather_sems():
    return [DMA((NC,)), DMA((NC,)), DMA((7, 4)), DMA((7, 4))]


def call_a(k, v, ids, cw, cot):
    return pl.pallas_call(
        kernel_a,
        out_shape=(
            SDS((NC, 2, TOK, W), BF),
            SDS((NH, 2, ROWS, W), BF),
            SDS((TOK, SLOTS), BF),
            SDS((TOK, SLOTS), BF),
            SDS((TOK, SLOTS), BF),
        ),
        in_specs=[VM] * 5,
        out_specs=(ANY, ANY, VM, VM, VM),
        scratch_shapes=[
            pltpu.VMEM((2, ROWS, W), BF),
            DMA((3,)),
            DMA((2, 2, 4)), DMA((2, 2, 4)), DMA((16,)), DMA((16,)), DMA, DMA,
            *gather_sems(),
        ],
        compiler_params=params(1, 40),
        name="gather_keys_place_cotangents",
    )(k, v, ids, cw, cot)


def call_b(att, w, res, gain, place):
    return pl.pallas_call(
        kernel_b,
        out_shape=(SDS((NH, 2, ROWS, W), BF), SDS((TOK, W), F32), SDS((TOK, TOK), F32)),
        in_specs=[VM] * 5,
        out_specs=(ANY, VM, VM),
        scratch_shapes=[
            pltpu.VMEM((NH, TOK, W), BF),
            pltpu.VMEM((NH, TOK, W), BF),
            pltpu.VMEM((NH, 8, TOK), F32),
            pltpu.VMEM((2, ROWS, W), BF),
            DMA,
            DMA((NH,)), DMA((NH,)), DMA((NH,)), DMA((NH,)),
            *gather_sems(),
        ],
        compiler_params=params(2, 40),
        name="project_norm_place",
    )(att, w, res, gain, place)


def call_c(*args):
    return pl.pallas_call(
        kernel_c,
        out_shape=(
            SDS((TOK, W), BF), SDS((TOK, W), BF), SDS((TOK, W), BF), SDS((8, W), F32), SDS((TOK, TOP), F32),
            SDS((2, FD, D), BF), SDS((2, FD, D), BF), SDS((2, FD, D), BF),
        ),
        in_specs=[VM] * 14,
        out_specs=(VM,) * 8,
        scratch_shapes=[
            pltpu.VMEM((2, ROWS, FD), BF), pltpu.VMEM((2, ROWS, FD), BF), pltpu.VMEM((2, ROWS, FD), BF),
            pltpu.VMEM((2, ROWS, FD), F32), pltpu.VMEM((2, ROWS, FD), F32),
            pltpu.VMEM((2, NH, 2, ROWS, W), BF),
            pltpu.VMEM((8, 7, ROWS // 2, W), BF),
            pltpu.VMEM((2, 2, ROWS, W), BF),
            pltpu.VMEM((2, 2, NC, CAP, W), BF),
            pltpu.VMEM((NH, 8, TOK), F32),
            pltpu.VMEM((NH, TOK, W), BF),
            pltpu.VMEM((NC, 8, W), F32),
            DMA,
            DMA((7, 8)), DMA((7, 8)), DMA((2, 2)), DMA((2, 2)),
            DMA((NH,)), DMA((NH,)), DMA((NH,)), DMA((NH,)), DMA((NC,)), DMA((NC,)),
        ],
        compiler_params=params(3, 58),
        name="experts_reduce_return",
    )(*args)


def attend(q, kv, i):
    outs = []
    pos = i * TOK + jnp.arange(TOK, dtype=jnp.int32)
    allowed = pos[:, None] >= jnp.arange(NC * TOK, dtype=jnp.int32)[None, :]
    for n in range(2):
        cs = slice(n * DH, (n + 1) * DH)
        k = kv[:, 0, :, cs].reshape(NC * TOK, DH)
        v = kv[:, 1, :, cs].reshape(NC * TOK, DH)
        s = jnp.dot(q[:, cs], k.T, preferred_element_type=F32) * DH ** (-0.5)
        top = jnp.max(jnp.where(allowed, s, -1e30), axis=1, keepdims=True)
        wts = jnp.where(allowed, jnp.exp(s - top), 0.0)
        tot = jnp.sum(wts, axis=1, keepdims=True)
        outs.append(jnp.dot(wts.astype(BF), v, preferred_element_type=F32) / tot)
    return jnp.concatenate(outs, axis=1).astype(BF)


def per_device(queries, key_rows, value_rows, output_weight, residual_stream, norm_gain, expert_ids,
               combine_weights, gate_weight, up_weight, down_weight, cotangent):
    i = lax.axis_index("ctx")
    gain = norm_gain.reshape(1, W)
    kv, gcot, place, whi, wlo = call_a(key_rows, value_rows, expert_ids, combine_weights, cotangent)
    att = attend(queries, kv, i)
    gin, normed, inv = call_b(att, output_weight, residual_stream, gain, place)
    moe, attg, resg, gaing, combg, dgate, dup, ddown = call_c(
        gin, gcot, gate_weight, up_weight, down_weight, expert_ids, place, whi, wlo, cotangent,
        normed, inv, gain, output_weight)
    return moe, attg, resg, gaing[0], combg, dgate, dup, ddown


def solution(mesh):
    return jax.shard_map(
        per_device,
        mesh=mesh,
        in_specs=(
            P("ctx", "head"), P("ctx", "head"), P("ctx", "head"), P("head", None), P("ctx", "head"), P("head"),
            P("ctx", None), P("ctx", None), P("ctx", "head", None), P("ctx", "head", None),
            P("ctx", "head", None), P("ctx", "head"),
        ),
        out_specs=(
            P("ctx", "head"), P("ctx", "head"), P("ctx", "head"), P("head"), P("ctx", None),
            P("ctx", "head", None), P("ctx", "head", None), P("ctx", "head", None),
        ),
        check_vma=False,
    )
```

time: 730 us -> 263 us (0.36)
  waiting for transfers between devices: 349 us -> 0 us
  Pallas kernels: 0 us -> 234 us
  blocking collectives: 205 us -> 0 us
  starting transfers between devices: 37.7 us -> 0 us
  local copies, waits for them, and re-layouts: 58.7 us -> 22.9 us
  matrix products: 29.5 us -> 2.87 us
  other arithmetic: 26.2 us -> 0.58 us
  between operations: 15 us -> 0.8 us
    pallas_call x0 -> x3, Pallas kernels: none -> 234 us  [the longest x1 99.8 us: call_c(): pl.pallas_call(kernel_c, out_shape=(SDS((TOK, W), BF), SDS((TOK, W), BF),...]
    reduce_scatter x3 -> x0, waiting for transfers between devices: 134 us -> none  [the longest x2 95.2 us: collect(): lax.psum_scatter(partial_value.astype(jnp.bfloat16), 'head', scatter_dime...]
    psum x3 -> x0, blocking collectives: 118 us -> none  [the longest x1 65.6 us: per_device(): gain_grad = lax.psum(jnp.sum(input_grad * normed, axis=0), 'ctx')]
    all_gather x2 -> x0, waiting for transfers between devices: 115 us -> none  [the longest x1 95.9 us: attend(): value_part = lax.all_gather(value_rows, 'ctx', axis=0, tiled=True)]
    all_to_all x4 -> x0, waiting for transfers between devices: 99.5 us -> none  [the longest x2 91.9 us: deliver(): lax.all_to_all(packed, 'ctx', split_axis=0, concat_axis=1, tiled=True)]
    all_gather x3 -> x0, blocking collectives: 87.3 us -> none  [the longest x2 58.5 us: deliver(): whole = lax.all_gather(local_rows, 'head', axis=1, tiled=True)]
    all_to_all x4 -> x0, starting transfers between devices: 37.3 us -> none  [the longest x2 19.3 us: deliver(): lax.all_to_all(packed, 'ctx', split_axis=0, concat_axis=1, tiled=True)]
    dot_general x12 -> x4, matrix products: 28 us -> 2.87 us  [the longest x2 1.54 us: attend(): s = jnp.dot(q[:, cs], k.T, preferred_element_type=F32) * DH ** (-0.5)]
  transfers between devices with their start and end apart: 9 -> 0, of which waited for: 7 -> 0; matrix products, arithmetic and copies ran while one was open for 12% -> 0% of each run, Pallas kernels for 0% -> 0%
where the time goes in v1:
time: 263 us; the launch traced here: 261 us
  Pallas kernels  234 us (89%)
  local copies, waits for them, and re-layouts  22.9 us (9%)
  matrix products  2.87 us (1%)
    pallas_call x1, Pallas kernels, call_c(): pl.pallas_call(kernel_c, out_shape=(SDS((TOK, W), BF), SDS((TOK, W), BF),...  99.8 us
    pallas_call x1, Pallas kernels, call_b(): pl.pallas_call(kernel_b, out_shape=(SDS((NH, 2, ROWS, W), BF), SDS((TOK,...  69.1 us
    pallas_call x1, Pallas kernels, call_a(): pl.pallas_call(kernel_a, out_shape=(SDS((NC, 2, TOK, W), BF), SDS((NH, 2,...  64.8 us
    unnamed x43, local copies, waits for them, and re-layouts  20.3 us

profile of v1, /device:TPU:2, one launch (start us, length us, event | category | flops | bytes accessed | tf_op | source)
XLA Modules:
  0.0 260.8 jit_solution(14631538923779379838)
XLA Ops:
  0.6 0.8 copy.20.ids_ref
  1.4 0.0 copy-start.4
  1.4 0.8 copy.21.cw_ref
  2.3 0.0 copy-start.7
  2.3 0.8 copy-done.7
  3.1 0.0 copy-start.10
  3.1 0.8 copy-done.10
  4.0 0.8 copy-done.11
  4.8 64.8 %gather_keys_place_cotangents.1 = (bf16[32,2,128,256]{3,2,1,0:T(8,128)(2,1)S(1)}, bf16[8,2,512,256]{3,2,1,0:T(8,128)(2,1)S(1)}, bf16[128,1024]{1,0:T(8,128)(2,1)...) custom-call(bf16[128,256]{1,0:T(8,128)(2,1)S(1)} %copy-done.10, bf16[128,256]{1,0:T(8,128)(2,1)S(1)} %copy-done.11, ...), custom_call_target="tpu_custom_call" | custom-call | tf_op jit(solution)/shard_map/gather_keys_place_cotangents/pallas_call | solution.py:531
  69.6 0.0 copy-start.1
  69.6 0.0 copy-start.5
  69.6 0.0 copy-start.6
  69.6 0.0 copy-start.3
  69.6 0.0 copy-start.16
  69.7 1.2 fusion.20
  70.9 0.0 copy-done.4
  70.9 0.7 copy-done.1
  71.6 0.1 copy-done.5
  71.7 0.1 copy-done.6
  71.8 0.0 copy-done.16
  71.8 0.7 select_reduce_fusion.1
  72.5 0.8 fusion.2
  73.3 0.7 fusion.6
  74.0 0.6 fusion.4
  74.5 0.0 copy-start.12
  74.6 0.0 copy-start.13
  74.6 0.7 fusion.7
  75.2 0.0 copy-done.3
  75.3 0.5 copy-done
  75.8 0.0 copy-done.12
  75.8 0.0 copy-done.13
  75.8 69.1 %project_norm_place.1 = (bf16[8,2,512,256]{3,2,1,0:T(8,128)(2,1)S(1)}, f32[128,256]{1,0:T(8,128)S(1)}, f32[128,128]{1,0:T(8,128)S(1)}) custom-call(bf16[128,256]{1,0:T(8,128)(2,1)S(1)} %pad_maximum_fusion.att, bf16[256,2048]{1,0:T(8,128)(2,1)S(1)} %copy-done, bf16[128,256]{1,0:T(8,128)(2,1)S(1)} %copy-done.12, f32[1,256]{1,0:T(1,128)S(1)} %bitcast.15, ...), custom_call_target="tpu_custom_call" | custom-call | tf_op jit(solution)/shard_map/project_norm_place/pallas_call | solution.py:554
  144.8 0.0 copy-start.2
  144.9 1.9 copy-done.2
  146.8 0.6 copy-done.8
  147.5 0.6 copy-done.9
  148.1 99.8 %experts_reduce_return.1 = (bf16[128,256]{1,0:T(8,128)(2,1)}, bf16[128,256]{1,0:T(8,128)(2,1)}, bf16[128,256]{1,0:T(8,128)(2,1)}, f32[8,256]{1,0:T(8,128)}, f32[...) custom-call(bf16[8,2,512,256]{3,2,1,0:T(8,128)(2,1)} %copy-done.2, ...), custom_call_target="tpu_custom_call" | custom-call | tf_op jit(solution)/shard_map/experts_reduce_return/pallas_call | solution.py:574
  247.8 0.0 copy-start.15
  247.9 1.4 slice.27
  249.2 1.5 copy.25
  250.7 1.5 copy.34
  252.2 1.5 copy.35
  253.7 1.5 copy.36
  255.1 2.6 %copy.37 = bf16[2,176,2048]{2,1,0:T(8,128)(2,1)} copy(bf16[2,176,2048]{2,1,0:T(8,128)(2,1)} %get-tuple-element.70) | data formatting | bytes 2883584
  257.8 0.0 copy-done.15
  257.8 1.1 copy.38
  258.9 0.8 copy-done.14
  259.7 1.1 copy.39
  (7 shorter events, 0.0 us)
Async XLA Ops:
  1.4 69.4 %copy-start.4 = (s32[128,6]{1,0:T(8,128)}, s32[128,6]{1,0:T(8,128)S(1)}, u32[]{:S(2)}) copy-start(s32[128,6]{1,0:T(8,128)S(1)} %copy.20.ids_ref) | copy-start | bytes 9220
  2.3 0.8 copy-start.7
  3.1 0.8 copy-start.10
  3.9 0.8 copy-start.11
  69.6 2.0 copy-start.1
  69.6 2.1 copy-start.5
  69.6 2.1 copy-start.6
  69.6 5.6 %copy-start.3 = (bf16[128,1024]{1,0:T(8,128)(2,1)}, bf16[128,1024]{1,0:T(8,128)(2,1)S(1)}, u32[]{:S(2)}) copy-start(bf16[128,1024]{1,0:T(8,128)(2,1)S(1)} %get-tuple-element.25.place) | copy-start | bytes 786436
  69.6 2.1 copy-start.16
  74.5 1.2 copy-start
  74.5 1.2 copy-start.12
  74.6 1.2 copy-start.13
  144.8 2.0 copy-start.2
  146.8 0.7 copy-start.8
  147.5 0.6 copy-start.9
  247.8 9.9 %copy-start.15 = (bf16[2,176,2048]{2,1,0:T(8,128)(2,1)S(1)}, bf16[2,176,2048]{2,1,0:T(8,128)(2,1)}, u32[]{:S(2)}) copy-start(bf16[2,176,2048]{2,1,0:T(8,128)(2,1)} %get-tuple-element.71) | copy-start | bytes 4325380
  257.8 1.9 copy-start.14

commit v2 on v1

v2 whole, which is shorter than its diff:
```python
import jax
import jax.numpy as jnp
from jax import lax
from jax.experimental import pallas as pl
from jax.experimental.pallas import tpu as pltpu
from jax.sharding import PartitionSpec as P

D = 2048
TOP = 6
DH = 128
NC = 32
NH = 8
TOK = 128
W = 256
FD = 176
CAP = 16
ROWS = NC * CAP
SLOTS = 2 * ROWS
MESH = pl.DeviceIdType.MESH
BF = jnp.bfloat16
F32 = jnp.float32


def dot(a, b, ca=1, cb=0):
    return lax.dot_general(a, b, (((ca,), (cb,)), ((), ())), preferred_element_type=F32)


def coords():
    return lax.axis_index("ctx"), lax.axis_index("head")


def head_of(xl, y):
    return xl * 4 + lax.rem(y + 4, 4)


def ctx_of(xh, z, core):
    return xh * 16 + lax.rem(z + 8, 8) * 2 + core


def remote(src, dst, ssem, rsem, ctx, head):
    return pltpu.make_async_remote_copy(
        src, dst, ssem, rsem, device_id=(ctx, head), device_id_type=MESH
    )


def greet():
    i, h = coords()
    bar = pltpu.get_barrier_semaphore()

    def ctx_peer(o, c):
        pl.semaphore_signal(bar, 1, device_id=(lax.rem(i + o, NC), h), device_id_type=MESH)
        return c

    def head_peer(o, c):
        pl.semaphore_signal(bar, 1, device_id=(i, lax.rem(h + o, NH)), device_id_type=MESH)
        return c

    lax.fori_loop(1, NC, ctx_peer, 0)
    lax.fori_loop(1, NH, head_peer, 0)
    pl.semaphore_wait(bar, NC - 1 + NH - 1)


def routing(ids, cw):
    eio = lax.broadcasted_iota(jnp.int32, (TOK, 2 * NC), 1)
    hot = jnp.zeros((TOK, 2 * NC), F32)
    wts = jnp.zeros((TOK, 2 * NC), F32)
    for k in range(TOP):
        m = ids[:, k : k + 1] == eio
        hot = hot + jnp.where(m, 1.0, 0.0)
        wts = wts + jnp.where(m, cw[:, k : k + 1], 0.0)
    r = lax.broadcasted_iota(jnp.int32, (TOK, TOK), 0)
    c = lax.broadcasted_iota(jnp.int32, (TOK, TOK), 1)
    lower = jnp.where(c < r, 1.0, 0.0).astype(BF)
    earlier = dot(lower, hot.astype(BF))
    n = lax.broadcasted_iota(jnp.int32, (2 * NC, SLOTS), 1)
    e = lax.broadcasted_iota(jnp.int32, (2 * NC, SLOTS), 0)
    spread = jnp.where(e == 2 * (lax.rem(n, ROWS) // CAP) + n // ROWS, 1.0, 0.0).astype(BF)
    hot_n = dot(hot.astype(BF), spread)
    earlier_n = dot(earlier.astype(BF), spread)
    slot = lax.rem(lax.broadcasted_iota(jnp.int32, (TOK, SLOTS), 1), CAP).astype(F32)
    place = jnp.where((hot_n > 0.5) & (earlier_n == slot), 1.0, 0.0)
    hi = wts.astype(BF)
    lo = (wts - hi.astype(F32)).astype(BF)
    whi = place * dot(hi, spread)
    wlo = place * dot(lo, spread)
    return place.astype(BF), whi.astype(BF), wlo.astype(BF)


def start_dispatch(packed, g, asend, arecv, lsem):
    i, h = coords()
    mine = pl.ds(pl.multiple_of(i * CAP, CAP), CAP)

    for e in range(2):

        def send(o, c):
            d = lax.rem(i + o, NC)
            theirs = pl.ds(pl.multiple_of(d * CAP, CAP), CAP)
            remote(packed.at[e, theirs], g.at[h, e, mine], asend.at[e], arecv.at[e], d, h).start()
            return c

        lax.fori_loop(1, NC, send, 0)
    own = pltpu.make_async_copy(packed.at[:, mine], g.at[h, :, mine], lsem)
    own.start()
    own.wait()


def dispatched(packed, g, asend, arecv, e):
    i, h = coords()
    most = pl.ds(0, (NC - 1) * CAP)
    return remote(packed.at[e, most], g.at[h, e, most], asend.at[e], arecv.at[e], i, 7 - h)


def gather_flow(g, gate, ssem, rsem, done):
    i, h = coords()
    xl, y = h // 4, lax.rem(h, 4)
    xp, up, down = head_of(1 - xl, y), head_of(xl, y + 1), head_of(xl, y - 1)
    pup, pdown = head_of(1 - xl, y + 1), head_of(1 - xl, y - 1)
    far, pfar = head_of(xl, y + 2), head_of(1 - xl, y + 2)
    half_rows = ROWS // 2
    chunks = [(e, hf) for e in range(2) for hf in range(2)]

    def copy(kind, c, block, target):
        e, hf = c
        view = g.at[block, e, pl.ds(hf * half_rows, half_rows)]
        n = e * 2 + hf
        return remote(view, view, ssem.at[kind, n], rsem.at[kind, n], i, target)

    def own(n):
        e, hf = chunks[n]
        if hf == 0:
            gate(e)
        copy(0, chunks[n], h, xp).start()
        copy(1, chunks[n], h, up).start()
        copy(2, chunks[n], h, down).start()

    own(0)
    for n in range(7):
        if n + 1 < 4:
            own(n + 1)
        yield
        if 0 <= n < 4:
            c = chunks[n]
            copy(0, c, xp, xp).wait_recv()
            copy(3, c, xp, up).start()
            copy(4, c, xp, down).start()
            if c[1] == 0:
                copy(1, c, down, up).wait_recv()
                copy(5, c, down, up).start()
            else:
                copy(2, c, up, down).wait_recv()
                copy(5, c, up, down).start()
        if 0 <= n - 1 < 4:
            c = chunks[n - 1]
            copy(5, c, far, up).wait_recv()
            copy(6, c, far, xp).start()
        if 0 <= n - 2 < 4:
            c = chunks[n - 2]
            if c[1] == 0:
                copy(2, c, up, up).wait_recv()
            else:
                copy(1, c, down, up).wait_recv()
            copy(3, c, pdown, up).wait_recv()
            copy(4, c, pup, up).wait_recv()
            copy(6, c, pfar, up).wait_recv()
            done(n - 2)
    for c in chunks:
        copy(0, c, h, xp).wait_send()
        copy(1, c, h, up).wait_send()
        copy(2, c, h, down).wait_send()
        copy(3, c, xp, up).wait_send()
        copy(4, c, xp, down).wait_send()
        copy(5, c, down, up).wait_send()
        copy(6, c, far, xp).wait_send()


def key_flow(kv, zs, zr, ks, kr):
    i, h = coords()
    xh, z, core = i // 16, lax.rem(i // 2, 8), lax.rem(i, 2)
    up, down = ctx_of(xh, z + 1, core), ctx_of(xh, z - 1, core)
    twin = ctx_of(xh, z, 1 - core)
    lanes = [(k, d) for k in range(2) for d in range(2)]

    def hops(k, d):
        return 4 if k == d else 3

    def view(k, dz, c):
        return kv.at[lax.rem(z + dz + 8, 8) * 2 + c, k]

    def ring(k, d, s):
        v = view(k, -s if d == 0 else s, core)
        return remote(v, v, zs.at[k, d, s], zr.at[k, d, s], up if d == 0 else down, h)

    def landed(k, d, s):
        v = view(k, -s - 1 if d == 0 else s + 1, core)
        return remote(v, v, zs.at[k, d, s], zr.at[k, d, s], up if d == 0 else down, h)

    def share(k, dz, c):
        v = view(k, dz, c)
        return remote(v, v, ks.at[k, dz % 8], kr.at[k, dz % 8], twin, h)

    for k, d in lanes:
        ring(k, d, 0).start()
    for k in range(2):
        share(k, 0, core).start()
    yield
    for s in range(4):
        for k, d in lanes:
            if s < hops(k, d):
                landed(k, d, s).wait_recv()
                if s + 1 < hops(k, d):
                    ring(k, d, s + 1).start()
                share(k, -s - 1 if d == 0 else s + 1, core).start()
        yield
    for k in range(2):
        for dz in range(-4, 4):
            share(k, dz, 1 - core).wait_recv()
    yield
    for k, d in lanes:
        for s in range(hops(k, d)):
            ring(k, d, s).wait_send()
    for k in range(2):
        for dz in range(-4, 4):
            share(k, dz, core).wait_send()
    yield


def to_rows(columns):
    lane = lax.broadcasted_iota(jnp.int32, (TOK, TOK), 1)
    packed = jnp.zeros((TOK, TOK), F32)
    for k, c in enumerate(columns):
        packed = jnp.where(lane == k, c, packed)
    return packed.T[0:8]


def to_columns(rows):
    return jnp.concatenate([rows, jnp.zeros((TOK - 8, TOK), F32)], axis=0).T


def layer_kernel(q_in, k_in, v_in, w_in, res_in, gain, ids_in, cw_in, wg_in, wu_in, wd_in, cot_in,
                 moe_out, attg_out, resg_out, gaing_out, combg_out, dgate_out, dup_out, ddown_out,
                 qb, kv, w_ref, res, ids_ref, cw_ref, wg, wu, wd, cot_ref,
                 place, whi, wlo, packed, gcot, gin, ob, os, terms, got, stats, stats2, normed, inv,
                 act_s, gd_s, ud_s, gp_s, up_s, t_ref, r_ref, fin, picked, rgb, gsum,
                 moe, attg, resg, gaing, combg, dgate, dup, ddown,
                 lsem, osem, zs, zr, ks, kr, xs, xr, asend, arecv, gs, gr, ts, tr, ss, sr,
                 fs, fr, bs, br, rs, rr, qs, qr):
    i, h = coords()
    xh, z, core = i // 16, lax.rem(i // 2, 8), lax.rem(i, 2)
    xl, y = h // 4, lax.rem(h, 4)
    xp, up, down = head_of(1 - xl, y), head_of(xl, y + 1), head_of(xl, y - 1)
    pup, pdown = head_of(1 - xl, y + 1), head_of(1 - xl, y - 1)
    far, pfar = head_of(xl, y + 2), head_of(1 - xl, y + 2)
    other = ctx_of(1 - xh, z, core)
    HR = ROWS // 2
    seat = lax.rem(i, 16)

    loads = [
        pltpu.make_async_copy(s, d, lsem.at[n])
        for n, (s, d) in enumerate((
            (k_in, kv.at[seat, 0]), (v_in, kv.at[seat, 1]), (q_in, qb.at[0]), (ids_in, ids_ref), (cw_in, cw_ref),
            (cot_in, cot_ref), (w_in, w_ref), (res_in, res), (wg_in, wg), (wu_in, wu), (wd_in, wd),
        ))
    ]
    for c in loads:
        c.start()
    greet()
    for c in loads[0:3]:
        c.wait()

    keys = key_flow(kv, zs, zr, ks, kr)
    next(keys)
    q_swap = remote(qb.at[0], qb.at[1], xs.at[0], xr.at[0], other, h)
    q_swap.start()
    for c in loads[3:6]:
        c.wait()
    pad = jnp.zeros((TOK - TOP, TOK), F32)
    ids = jnp.concatenate([ids_ref[...].astype(F32), pad], axis=0).T.astype(jnp.int32)
    cw = jnp.concatenate([cw_ref[...], pad], axis=0).T
    p, hi, lo = routing(ids, cw)
    place[...] = p
    whi[...] = hi
    wlo[...] = lo
    next(keys)
    cot = cot_ref[...]
    rows = dot(hi, cot, 0, 0) + dot(lo, cot, 0, 0)
    packed[0] = rows.astype(BF).reshape(2, ROWS, W)
    next(keys)
    next(keys)
    start_dispatch(packed.at[0], gcot, asend.at[0], arecv.at[0], lsem.at[11])
    next(keys)
    next(keys)

    q_swap.wait_recv()
    q2 = jnp.concatenate([qb[0], qb[1]], axis=0)
    r = lax.broadcasted_iota(jnp.int32, (2 * TOK, 1), 0)
    limit = jnp.where(r < TOK, seat * TOK + r, jnp.where(xh == 0, 16 * TOK - 1, -1))
    allowed = lax.broadcasted_iota(jnp.int32, (2 * TOK, 16 * TOK), 1) <= limit
    outs, tops, sums = [], [], []
    for n in range(2):
        cs = slice(n * DH, (n + 1) * DH)
        s = dot(q2[:, cs], kv[:, 0, :, cs].reshape(16 * TOK, DH), 1, 1) * DH ** (-0.5)
        s = jnp.where(allowed, s, -1e30)
        m = jnp.max(s, axis=1, keepdims=True)
        wts = jnp.exp(s - m)
        tot = jnp.sum(wts, axis=1, keepdims=True)
        o = dot(wts.astype(BF), kv[:, 1, :, cs].reshape(16 * TOK, DH)) / tot
        outs.append(o)
        tops.append(m)
        sums.append(tot)
    seen = jnp.where(xh == 0, 1.0, 0.0)
    ob[0] = jnp.concatenate([o[TOK:] for o in outs], axis=1).astype(BF)
    os[0] = to_rows([tops[0][TOK:], sums[0][TOK:] * seen, tops[1][TOK:], sums[1][TOK:] * seen])
    o_swap = remote(ob.at[0], ob.at[1], xs.at[1], xr.at[1], other, h)
    s_swap = remote(os.at[0], os.at[1], xs.at[2], xr.at[2], other, h)
    o_swap.start()
    s_swap.start()
    loads[6].wait()
    loads[7].wait()
    s_swap.wait_recv()
    o_swap.wait_recv()
    there = to_columns(os[1])
    att = []
    for n in range(2):
        m1, l1 = tops[n][:TOK], sums[n][:TOK]
        m2, l2 = there[:, 2 * n : 2 * n + 1], there[:, 2 * n + 1 : 2 * n + 2]
        m = jnp.maximum(m1, m2)
        a1, a2 = l1 * jnp.exp(m1 - m), l2 * jnp.exp(m2 - m)
        o2 = ob[1, :, n * DH : (n + 1) * DH].astype(F32)
        att.append((a1 * outs[n][:TOK] + a2 * o2) / (a1 + a2))
    att = jnp.concatenate(att, axis=1).astype(BF)

    t = dot(att, w_ref[...]).astype(BF)
    for d in range(NH):
        terms[d] = t[:, d * W : (d + 1) * W]
    for o in range(1, NH):
        d = lax.rem(h + o, NH)
        remote(terms.at[d], got.at[o], ts.at[o], tr.at[o], i, d).start()

    cots = gather_flow(gcot, lambda e: dispatched(packed.at[0], gcot, asend.at[0], arecv.at[0], e).wait_recv(),
                       gs.at[0], gr.at[0], lambda n: None)
    next(cots)
    hidden = res[...].astype(F32) + terms[h].astype(F32)
    for o in range(1, NH):
        d = lax.rem(h + o, NH)
        remote(terms.at[d], got.at[o], ts.at[o], tr.at[o], i, d).wait()
        hidden = hidden + got[o].astype(F32)
    stats[0] = to_rows([jnp.sum(hidden * hidden, axis=1, keepdims=True)])
    for o in range(1, NH):
        remote(stats.at[0], stats.at[o], ss.at[0, o], sr.at[0, o], i, lax.rem(h + o, NH)).start()
    next(cots)
    total = stats[0]
    for o in range(1, NH):
        remote(stats.at[0], stats.at[o], ss.at[0, o], sr.at[0, o], i, lax.rem(h + o, NH)).wait()
        total = total + stats[o]
    inverse = lax.rsqrt(to_columns(total)[:, 0:1] / D + 1e-06)
    inv[...] = jnp.broadcast_to(inverse, (TOK, TOK))
    nrm = hidden * inverse
    normed[...] = nrm
    inputs = (nrm * gain[...]).astype(BF)
    packed[1] = dot(place[...], inputs, 0, 0).astype(BF).reshape(2, ROWS, W)
    start_dispatch(packed.at[1], gin, asend.at[1], arecv.at[1], lsem.at[11])
    for _ in cots:
        pass
    for c in loads[8:]:
        c.wait()

    def rows_of(ref, e, lo, n):
        return jnp.concatenate([ref[b, e, lo : lo + n] for b in range(NH)], axis=1)

    def forward(e, hf):
        sl = slice(hf * HR, (hf + 1) * HR)
        x = rows_of(gin, e, hf * HR, HR)
        gp = dot(x, wg[e], 1, 1)
        u = dot(x, wu[e], 1, 1)
        gp_s[e, sl] = gp
        up_s[e, sl] = u
        act = (gp * jax.nn.sigmoid(gp) * u).astype(BF)
        act_s[e, sl] = act
        for b in range(NH):
            t_ref[0, b, e, sl] = dot(act, wd[e, :, b * W : (b + 1) * W]).astype(BF)

    def backward(e, hf):
        sl = slice(hf * HR, (hf + 1) * HR)
        x = rows_of(gcot, e, hf * HR, HR)
        ag = dot(x, wd[e], 1, 1)
        gp = gp_s[e, sl]
        s = jax.nn.sigmoid(gp)
        gd = (ag * up_s[e, sl] * s * (1.0 + gp * (1.0 - s))).astype(BF)
        ud = (ag * gp * s).astype(BF)
        gd_s[e, sl] = gd
        ud_s[e, sl] = ud
        for b in range(NH):
            cs = slice(b * W, (b + 1) * W)
            t_ref[1, b, e, sl] = (dot(gd, wg[e, :, cs]) + dot(ud, wu[e, :, cs])).astype(BF)

    def weight_grads(e):
        for b in range(NH):
            cs = slice(b * W, (b + 1) * W)
            x = gin[b, e]
            dgate[e, :, cs] = dot(gd_s[e], x, 0, 0).astype(BF)
            dup[e, :, cs] = dot(ud_s[e], x, 0, 0).astype(BF)
            ddown[e, :, cs] = dot(act_s[e], gcot[b, e], 0, 0).astype(BF)

    def tview(f, block):
        t, e, hf = f
        return t_ref.at[t, block, e, pl.ds(hf * HR, HR)]

    def copy(kind, f, block, target):
        n = f[0] * 4 + f[1] * 2 + f[2]
        return remote(tview(f, block), r_ref.at[n, kind], fs.at[kind, n], fr.at[kind, n], i, target)

    def add(f, block, kinds):
        n = f[0] * 4 + f[1] * 2 + f[2]
        v = tview(f, block)
        acc = v[...].astype(F32)
        for kind in kinds:
            acc = acc + r_ref[n, kind].astype(F32)
        return acc.astype(BF)

    def stage0(f):
        copy(0, f, pfar, xp).start()
        copy(1, f, pup, up).start()
        copy(2, f, pdown, down).start()
        if f[2] == 0:
            copy(6, f, down, down).start()
        else:
            copy(5, f, up, up).start()

    def stage1(f):
        copy(0, f, far, xp).wait_recv()
        tview(f, far)[...] = add(f, far, (0,))
        copy(3, f, far, up if f[2] == 0 else down).start()
        copy(1, f, xp, up).wait_recv()
        copy(2, f, xp, up).wait_recv()
        tview(f, xp)[...] = add(f, xp, (1, 2))
        copy(4, f, xp, xp).start()

    def stage2(f):
        block = up if f[2] == 0 else down
        copy(3, f, block, up).wait_recv()
        tview(f, block)[...] = add(f, block, (3,))
        copy(5 if f[2] == 0 else 6, f, block, block).start()

    def stage3(f):
        t, e, hf = f
        for kind in (4, 5, 6):
            copy(kind, f, h, up).wait_recv()
        fin[t, e, hf * HR : (hf + 1) * HR] = add(f, h, (4, 5, 6))

        def send(k, c):
            d = hf * 16 + k

            @pl.when(d != i)
            def _():
                back(t, e, d).start()

            return c

        lax.fori_loop(0, 16, send, 0)

    def back(t, e, d):
        return remote(fin.at[t, e, pl.ds(pl.multiple_of(d * CAP, CAP), CAP)], picked.at[t, e, i],
                      bs.at[t, e], br.at[t, e], d, h)

    def drain(f):
        for kind, block in ((0, pfar), (1, pup), (2, pdown), (3, far), (4, xp), (5, up), (6, down)):
            copy(kind, f, block, xp).wait_send()

    flows = [(t, e, hf) for t in range(2) for e in range(2) for hf in range(2)]
    outward = [
        pltpu.make_async_copy(s, d, osem.at[n])
        for n, (s, d) in enumerate((
            (moe, moe_out), (attg, attg_out), (resg, resg_out), (gaing, gaing_out), (combg, combg_out),
            (dgate, dgate_out), (dup, dup_out), (ddown, ddown_out),
        ))
    ]

    def tick(n):
        if n < len(flows):
            t, e, hf = flows[n]
            (forward if t == 0 else backward)(e, hf)
            stage0(flows[n])
        elif n == len(flows):
            weight_grads(0)
        elif n == len(flows) + 1:
            weight_grads(1)
            for c in outward[5:]:
                c.start()
        if 0 <= n - 1 < len(flows):
            stage1(flows[n - 1])
        if 0 <= n - 2 < len(flows):
            stage2(flows[n - 2])
        if 0 <= n - 3 < len(flows):
            stage3(flows[n - 3])

    for _ in gather_flow(gin, lambda e: dispatched(packed.at[1], gin, asend.at[1], arecv.at[1], e).wait_recv(),
                         gs.at[1], gr.at[1], tick):
        pass
    for n in range(4, len(flows) + 3):
        tick(n)

    def landed(t):
        mine = pl.ds(pl.multiple_of(i * CAP, CAP), CAP)
        for e in range(2):
            own = pltpu.make_async_copy(fin.at[t, e, mine], picked.at[t, e, i], lsem.at[11])
            own.start()
            own.wait()
            part = picked.at[t, e, pl.ds(0, NC - 1)]
            remote(part, part, bs.at[t, e], br.at[t, e], i, xp).wait()
        return picked[t].reshape(SLOTS, W)

    rows = landed(0)
    moe[...] = (dot(whi[...], rows) + dot(wlo[...], rows)).astype(BF)
    outward[0].start()
    every = dot(cot_ref[...], rows, 1, 1) * place[...].astype(F32)
    n = lax.broadcasted_iota(jnp.int32, (TOK, SLOTS), 1)
    expert = 2 * (lax.rem(n, ROWS) // CAP) + n // ROWS
    columns = [
        jnp.sum(jnp.where(expert == ids[:, k : k + 1], every, 0.0), axis=1, keepdims=True) for k in range(TOP)
    ]

    rows = landed(1)
    input_grad = dot(place[...], rows)
    nrm = normed[...]
    gsum[0] = jnp.broadcast_to(jnp.sum(input_grad * nrm, axis=0, keepdims=True), (8, W))

    def gain_copy(o):
        d = lax.rem(i + o, NC)
        return remote(gsum.at[0], gsum.at[o], qs.at[o], qr.at[o], d, h)

    def gain_start(o, c):
        gain_copy(o).start()
        return c

    ng = input_grad * gain[...]
    stats2[0] = to_rows(columns + [jnp.sum(ng * nrm, axis=1, keepdims=True)])
    for o in range(1, NH):
        remote(stats2.at[0], stats2.at[o], ss.at[1, o], sr.at[1, o], i, lax.rem(h + o, NH)).start()
    lax.fori_loop(1, NC, gain_start, 0)
    total = stats2[0]
    for o in range(1, NH):
        remote(stats2.at[0], stats2.at[o], ss.at[1, o], sr.at[1, o], i, lax.rem(h + o, NH)).wait()
        total = total + stats2[o]
    combg[...] = total[0:TOP]
    outward[4].start()
    centre = to_columns(total)[:, TOP : TOP + 1] / D
    rg = (inv[:, 0:1] * (ng - nrm * centre)).astype(BF)
    resg[...] = rg
    outward[2].start()
    rgb[h] = rg
    for o in range(1, NH):
        d = lax.rem(h + o, NH)
        remote(rgb.at[h], rgb.at[h], rs.at[o], rr.at[o], i, d).start()

    def gain_wait(o, c):
        gain_copy(o).wait()
        return c + gsum[o]

    gaing[...] = lax.fori_loop(1, NC, gain_wait, gsum[0])[0:1]
    outward[3].start()
    for f in flows:
        drain(f)
    for part in range(2):
        for e in range(2):
            dispatched(packed.at[part], (gcot, gin)[part], asend.at[part], arecv.at[part], e).wait_send()
    q_swap.wait_send()
    o_swap.wait_send()
    s_swap.wait_send()
    for _ in keys:
        pass
    for o in range(1, NH):
        s = lax.rem(h - o + NH, NH)
        remote(rgb.at[s], rgb.at[s], rs.at[o], rr.at[o], i, s).wait()
    whole = jnp.concatenate([rgb[b] for b in range(NH)], axis=1)
    attg[...] = dot(whole, w_ref[...], 1, 1).astype(BF)
    outward[1].start()
    for c in outward:
        c.wait()


VM = pl.BlockSpec(memory_space=pltpu.VMEM)
ANY = pl.BlockSpec(memory_space=pl.ANY)
DMA = pltpu.SemaphoreType.DMA
SDS = jax.ShapeDtypeStruct
RESULTS = (
    ((TOK, W), BF), ((TOK, W), BF), ((TOK, W), BF), ((1, W), F32), ((TOP, TOK), F32),
    ((2, FD, D), BF), ((2, FD, D), BF), ((2, FD, D), BF),
)


def call_layer(*args):
    v = pltpu.VMEM
    return pl.pallas_call(
        layer_kernel,
        out_shape=tuple(SDS(s, t) for s, t in RESULTS),
        in_specs=[ANY] * 5 + [VM] + [ANY] * 6,
        out_specs=(ANY,) * 8,
        scratch_shapes=[
            v((2, TOK, W), BF), v((16, 2, TOK, W), BF), v((W, D), BF), v((TOK, W), BF),
            v((TOP, TOK), jnp.int32), v((TOP, TOK), F32),
            v((2, FD, D), BF), v((2, FD, D), BF), v((2, FD, D), BF), v((TOK, W), BF),
            v((TOK, SLOTS), BF), v((TOK, SLOTS), BF), v((TOK, SLOTS), BF),
            v((2, 2, ROWS, W), BF), v((NH, 2, ROWS, W), BF), v((NH, 2, ROWS, W), BF),
            v((2, TOK, W), BF), v((2, 8, TOK), F32), v((NH, TOK, W), BF), v((NH, TOK, W), BF),
            v((NH, 8, TOK), F32), v((NH, 8, TOK), F32), v((TOK, W), F32), v((TOK, TOK), F32),
            v((2, ROWS, FD), BF), v((2, ROWS, FD), BF), v((2, ROWS, FD), BF),
            v((2, ROWS, FD), F32), v((2, ROWS, FD), F32),
            v((2, NH, 2, ROWS, W), BF), v((8, 7, ROWS // 2, W), BF), v((2, 2, ROWS, W), BF),
            v((2, 2, NC, CAP, W), BF), v((NH, TOK, W), BF), v((NC, 8, W), F32),
            *[v(s, t) for s, t in RESULTS],
            DMA((12,)), DMA((8,)),
            DMA((2, 2, 4)), DMA((2, 2, 4)), DMA((2, 8)), DMA((2, 8)), DMA((3,)), DMA((3,)),
            DMA((2, 2)), DMA((2, 2)), DMA((2, 7, 4)), DMA((2, 7, 4)), DMA((NH,)), DMA((NH,)),
            DMA((2, NH)), DMA((2, NH)),
            DMA((7, 8)), DMA((7, 8)), DMA((2, 2)), DMA((2, 2)), DMA((NH,)), DMA((NH,)), DMA((NC,)), DMA((NC,)),
        ],
        compiler_params=pltpu.CompilerParams(collective_id=1, has_side_effects=True, vmem_limit_bytes=60 << 20),
        name="layer",
    )(*args)


def hand_on(*args):
    parts = [(n, None) for n in range(5)] + [(n, e) for n in range(5, 8) for e in range(2)]

    def kernel(*refs):
        into, sems = refs[16:24], refs[24]

        def at(ref, e):
            return ref if e is None else ref.at[e]

        ins = [pltpu.make_async_copy(at(refs[n], e), at(into[n], e), sems.at[0, k]) for k, (n, e) in enumerate(parts)]
        outs = [pltpu.make_async_copy(at(into[n], e), at(refs[n + 8], e), sems.at[1, k]) for k, (n, e) in enumerate(parts)]
        for c in ins:
            c.start()
        for a, b in zip(ins, outs):
            a.wait()
            b.start()
        for c in outs:
            c.wait()

    return pl.pallas_call(
        kernel,
        out_shape=tuple(SDS(s, t) for s, t in RESULTS),
        in_specs=[ANY] * 8,
        out_specs=(ANY,) * 8,
        scratch_shapes=[pltpu.VMEM(s, t) for s, t in RESULTS] + [DMA((2, 11))],
        compiler_params=pltpu.CompilerParams(vmem_limit_bytes=60 << 20),
        name="hand_on",
    )(*args)


def per_device(queries, key_rows, value_rows, output_weight, residual_stream, norm_gain, expert_ids,
               combine_weights, gate_weight, up_weight, down_weight, cotangent):
    results = call_layer(
        queries, key_rows, value_rows, output_weight, residual_stream, norm_gain.reshape(1, W), expert_ids.T,
        combine_weights.T, gate_weight, up_weight, down_weight, cotangent)
    moe, attg, resg, gaing, combg, dgate, dup, ddown = hand_on(*results)
    return moe, attg, resg, gaing.reshape(W), combg.T, dgate, dup, ddown


def solution(mesh):
    return jax.shard_map(
        per_device,
        mesh=mesh,
        in_specs=(
            P("ctx", "head"), P("ctx", "head"), P("ctx", "head"), P("head", None), P("ctx", "head"), P("head"),
            P("ctx", None), P("ctx", None), P("ctx", "head", None), P("ctx", "head", None),
            P("ctx", "head", None), P("ctx", "head"),
        ),
        out_specs=(
            P("ctx", "head"), P("ctx", "head"), P("ctx", "head"), P("head"), P("ctx", None),
            P("ctx", "head", None), P("ctx", "head", None), P("ctx", "head", None),
        ),
        check_vma=False,
    )
```

time: 263 us -> 199 us (0.76)
  Pallas kernels: 234 us -> 197 us
  local copies, waits for them, and re-layouts: 22.9 us -> 0 us
  matrix products: 2.87 us -> 0 us
    pallas_call x3 -> x2, Pallas kernels: 234 us -> 197 us  [the longest x1 193 us: call_layer(): pl.pallas_call(layer_kernel, out_shape=tuple((SDS(s, t) for s, t in RESUL...]
    unnamed x43 -> x0, local copies, waits for them, and re-layouts: 20.3 us -> none
    dot_general x4 -> x0, matrix products: 2.87 us -> none  [the longest x2 1.54 us: attend(): s = jnp.dot(q[:, cs], k.T, preferred_element_type=F32) * DH ** (-0.5)]
where the time goes in v2:
time: 199 us; the launch traced here: 198 us
  Pallas kernels  197 us (99%)
    pallas_call x1, Pallas kernels, call_layer(): pl.pallas_call(layer_kernel, out_shape=tuple((SDS(s, t) for s, t in RESUL...  193 us
    pallas_call x1, Pallas kernels, hand_on(): pl.pallas_call(kernel, out_shape=tuple((SDS(s, t) for s, t in RESULTS)),...  3.99 us

profile of v2, /device:TPU:2, one launch (start us, length us, event | category | flops | bytes accessed | tf_op | source)
XLA Modules:
  0.0 197.8 jit_solution(5953192868105209901)
XLA Ops:
  0.6 193.0 %layer.1 = (bf16[128,256]{1,0:T(8,128)(2,1)}, bf16[128,256]{1,0:T(8,128)(2,1)}, bf16[128,256]{1,0:T(8,128)(2,1)}, f32[1,256]{1,0:T(1,128)}, f32[6,128]{1,0:T(8,1...) custom-call(bf16[128,256]{1,0:T(8,128)(2,1)} %q_in.1, ...), custom_call_target="tpu_custom_call" | custom-call | tf_op jit(solution)/shard_map/layer/pallas_call | solution.py:593
  193.7 4.0 %hand_on.1 = (bf16[128,256]{1,0:T(8,128)(2,1)}, bf16[128,256]{1,0:T(8,128)(2,1)}, bf16[128,256]{1,0:T(8,128)(2,1)}, f32[1,256]{1,0:T(1,128)}, f32[6,128]{1,0:T(8...) custom-call(bf16[128,256]{1,0:T(8,128)(2,1)} %get-tuple-element.24.refs_0_, ...), custom_call_target="tpu_custom_call" | custom-call | tf_op jit(solution)/shard_map/hand_on/pallas_call | solution.py:641

commit v3 on v2

--- a/solution.py
+++ b/solution.py
@@ -13,6 +13,8 @@
 TOK = 128
 W = 256
 FD = 176
+PART = 256
+PARTS = 2
 CAP = 16
 ROWS = NC * CAP
 SLOTS = 2 * ROWS
@@ -43,9 +45,8 @@
     )
 
 
-def greet():
+def greet(bar):
     i, h = coords()
-    bar = pltpu.get_barrier_semaphore()
 
     def ctx_peer(o, c):
         pl.semaphore_signal(bar, 1, device_id=(lax.rem(i + o, NC), h), device_id_type=MESH)
@@ -57,7 +58,6 @@
 
     lax.fori_loop(1, NC, ctx_peer, 0)
     lax.fori_loop(1, NH, head_peer, 0)
-    pl.semaphore_wait(bar, NC - 1 + NH - 1)
 
 
 def routing(ids, cw):
@@ -86,20 +86,18 @@
     return place.astype(BF), whi.astype(BF), wlo.astype(BF)
 
 
-def start_dispatch(packed, g, asend, arecv, lsem):
+def start_dispatch(packed, g, asend, arecv, lsem, e):
     i, h = coords()
     mine = pl.ds(pl.multiple_of(i * CAP, CAP), CAP)
 
-    for e in range(2):
-
-        def send(o, c):
-            d = lax.rem(i + o, NC)
-            theirs = pl.ds(pl.multiple_of(d * CAP, CAP), CAP)
-            remote(packed.at[e, theirs], g.at[h, e, mine], asend.at[e], arecv.at[e], d, h).start()
-            return c
-
-        lax.fori_loop(1, NC, send, 0)
-    own = pltpu.make_async_copy(packed.at[:, mine], g.at[h, :, mine], lsem)
+    def send(o, c):
+        d = lax.rem(i + o, NC)
+        theirs = pl.ds(pl.multiple_of(d * CAP, CAP), CAP)
+        remote(packed.at[e, theirs], g.at[h, e, mine], asend.at[e], arecv.at[e], d, h).start()
+        return c
+
+    lax.fori_loop(1, NC, send, 0)
+    own = pltpu.make_async_copy(packed.at[e, mine], g.at[h, e, mine], lsem)
     own.start()
     own.wait()
 
@@ -110,67 +108,60 @@
     return remote(packed.at[e, most], g.at[h, e, most], asend.at[e], arecv.at[e], i, 7 - h)
 
 
-def gather_flow(g, gate, ssem, rsem, done):
-    i, h = coords()
-    xl, y = h // 4, lax.rem(h, 4)
-    xp, up, down = head_of(1 - xl, y), head_of(xl, y + 1), head_of(xl, y - 1)
-    pup, pdown = head_of(1 - xl, y + 1), head_of(1 - xl, y - 1)
-    far, pfar = head_of(xl, y + 2), head_of(1 - xl, y + 2)
-    half_rows = ROWS // 2
-    chunks = [(e, hf) for e in range(2) for hf in range(2)]
-
-    def copy(kind, c, block, target):
-        e, hf = c
-        view = g.at[block, e, pl.ds(hf * half_rows, half_rows)]
-        n = e * 2 + hf
-        return remote(view, view, ssem.at[kind, n], rsem.at[kind, n], i, target)
-
-    def own(n):
-        e, hf = chunks[n]
-        if hf == 0:
-            gate(e)
-        copy(0, chunks[n], h, xp).start()
-        copy(1, chunks[n], h, up).start()
-        copy(2, chunks[n], h, down).start()
-
-    own(0)
-    for n in range(7):
-        if n + 1 < 4:
-            own(n + 1)
-        yield
-        if 0 <= n < 4:
-            c = chunks[n]
-            copy(0, c, xp, xp).wait_recv()
-            copy(3, c, xp, up).start()
-            copy(4, c, xp, down).start()
-            if c[1] == 0:
-                copy(1, c, down, up).wait_recv()
-                copy(5, c, down, up).start()
-            else:
-                copy(2, c, up, down).wait_recv()
-                copy(5, c, up, down).start()
-        if 0 <= n - 1 < 4:
-            c = chunks[n - 1]
-            copy(5, c, far, up).wait_recv()
-            copy(6, c, far, xp).start()
-        if 0 <= n - 2 < 4:
-            c = chunks[n - 2]
-            if c[1] == 0:
-                copy(2, c, up, up).wait_recv()
-            else:
-                copy(1, c, down, up).wait_recv()
-            copy(3, c, pdown, up).wait_recv()
-            copy(4, c, pup, up).wait_recv()
-            copy(6, c, pfar, up).wait_recv()
-            done(n - 2)
-    for c in chunks:
-        copy(0, c, h, xp).wait_send()
-        copy(1, c, h, up).wait_send()
-        copy(2, c, h, down).wait_send()
-        copy(3, c, xp, up).wait_send()
-        copy(4, c, xp, down).wait_send()
-        copy(5, c, down, up).wait_send()
-        copy(6, c, far, xp).wait_send()
+class HeadGather:
+    parts = [(e, q) for e in range(2) for q in range(PARTS)]
+
+    def __init__(self, g, ssem, rsem):
+        i, h = coords()
+        xl, y = h // 4, lax.rem(h, 4)
+        self.g, self.ssem, self.rsem, self.i, self.h = g, ssem, rsem, i, h
+        self.xp, self.up, self.down = head_of(1 - xl, y), head_of(xl, y + 1), head_of(xl, y - 1)
+        self.pup, self.pdown = head_of(1 - xl, y + 1), head_of(1 - xl, y - 1)
+        self.far, self.pfar = head_of(xl, y + 2), head_of(1 - xl, y + 2)
+
+    def copy(self, kind, n, block, target):
+        e, q = self.parts[n]
+        view = self.g.at[block, e, pl.ds(q * PART, PART)]
+        return remote(view, view, self.ssem.at[kind, n], self.rsem.at[kind, n], self.i, target)
+
+    def own(self, n):
+        self.copy(0, n, self.h, self.xp).start()
+        self.copy(1, n, self.h, self.up).start()
+        self.copy(2, n, self.h, self.down).start()
+
+    def pass_on(self, n):
+        self.copy(0, n, self.xp, self.xp).wait_recv()
+        self.copy(3, n, self.xp, self.up).start()
+        self.copy(4, n, self.xp, self.down).start()
+        if n % 2 == 0:
+            self.copy(1, n, self.down, self.up).wait_recv()
+            self.copy(5, n, self.down, self.up).start()
+        else:
+            self.copy(2, n, self.up, self.down).wait_recv()
+            self.copy(5, n, self.up, self.down).start()
+
+    def far_on(self, n):
+        self.copy(5, n, self.far, self.up).wait_recv()
+        self.copy(6, n, self.far, self.xp).start()
+
+    def whole(self, n):
+        if n % 2 == 0:
+            self.copy(2, n, self.up, self.up).wait_recv()
+        else:
+            self.copy(1, n, self.down, self.up).wait_recv()
+        self.copy(3, n, self.pdown, self.up).wait_recv()
+        self.copy(4, n, self.pup, self.up).wait_recv()
+        self.copy(6, n, self.pfar, self.up).wait_recv()
+
+    def drain(self):
+        for n in range(len(self.parts)):
+            self.copy(0, n, self.h, self.xp).wait_send()
+            self.copy(1, n, self.h, self.up).wait_send()
+            self.copy(2, n, self.h, self.down).wait_send()
+            self.copy(3, n, self.xp, self.up).wait_send()
+            self.copy(4, n, self.xp, self.down).wait_send()
+            self.copy(5, n, self.down, self.up).wait_send()
+            self.copy(6, n, self.far, self.xp).wait_send()
 
 
 def key_flow(kv, zs, zr, ks, kr):
@@ -263,14 +254,8 @@
     ]
     for c in loads:
         c.start()
-    greet()
-    for c in loads[0:3]:
-        c.wait()
-
-    keys = key_flow(kv, zs, zr, ks, kr)
-    next(keys)
-    q_swap = remote(qb.at[0], qb.at[1], xs.at[0], xr.at[0], other, h)
-    q_swap.start()
+    bar = pltpu.get_barrier_semaphore()
+    greet(bar)
     for c in loads[3:6]:
         c.wait()
     pad = jnp.zeros((TOK - TOP, TOK), F32)
@@ -280,14 +265,27 @@
     place[...] = p
     whi[...] = hi
     wlo[...] = lo
-    next(keys)
     cot = cot_ref[...]
     rows = dot(hi, cot, 0, 0) + dot(lo, cot, 0, 0)
     packed[0] = rows.astype(BF).reshape(2, ROWS, W)
+    for c in loads[0:3]:
+        c.wait()
+    pl.semaphore_wait(bar, NC - 1 + NH - 1)
+
+    def sent(part, g, e):
+        return dispatched(packed.at[part], g, asend.at[part], arecv.at[part], e)
+
+    keys = key_flow(kv, zs, zr, ks, kr)
+    next(keys)
+    q_swap = remote(qb.at[0], qb.at[1], xs.at[0], xr.at[0], other, h)
+    q_swap.start()
+    cots = HeadGather(gcot, gs.at[0], gr.at[0])
     next(keys)
     next(keys)
-    start_dispatch(packed.at[0], gcot, asend.at[0], arecv.at[0], lsem.at[11])
     next(keys)
+    start_dispatch(packed.at[0], gcot, asend.at[0], arecv.at[0], lsem.at[11], 0)
+    next(keys)
+    start_dispatch(packed.at[0], gcot, asend.at[0], arecv.at[0], lsem.at[11], 1)
     next(keys)
 
     q_swap.wait_recv()
@@ -314,6 +312,9 @@
     s_swap = remote(os.at[0], os.at[1], xs.at[2], xr.at[2], other, h)
     o_swap.start()
     s_swap.start()
+    sent(0, gcot, 0).wait_recv()
+    cots.own(0)
+    cots.own(1)
     loads[6].wait()
     loads[7].wait()
     s_swap.wait_recv()
@@ -336,9 +337,7 @@
         d = lax.rem(h + o, NH)
         remote(terms.at[d], got.at[o], ts.at[o], tr.at[o], i, d).start()
 
-    cots = gather_flow(gcot, lambda e: dispatched(packed.at[0], gcot, asend.at[0], arecv.at[0], e).wait_recv(),
-                       gs.at[0], gr.at[0], lambda n: None)
-    next(cots)
+    cots.pass_on(0)
     hidden = res[...].astype(F32) + terms[h].astype(F32)
     for o in range(1, NH):
         d = lax.rem(h + o, NH)
@@ -347,7 +346,11 @@
     stats[0] = to_rows([jnp.sum(hidden * hidden, axis=1, keepdims=True)])
     for o in range(1, NH):
         remote(stats.at[0], stats.at[o], ss.at[0, o], sr.at[0, o], i, lax.rem(h + o, NH)).start()
-    next(cots)
+    sent(0, gcot, 1).wait_recv()
+    cots.own(2)
+    cots.own(3)
+    cots.pass_on(1)
+    cots.far_on(0)
     total = stats[0]
     for o in range(1, NH):
         remote(stats.at[0], stats.at[o], ss.at[0, o], sr.at[0, o], i, lax.rem(h + o, NH)).wait()
@@ -358,9 +361,13 @@
     normed[...] = nrm
     inputs = (nrm * gain[...]).astype(BF)
     packed[1] = dot(place[...], inputs, 0, 0).astype(BF).reshape(2, ROWS, W)
-    start_dispatch(packed.at[1], gin, asend.at[1], arecv.at[1], lsem.at[11])
-    for _ in cots:
-        pass
+    start_dispatch(packed.at[1], gin, asend.at[1], arecv.at[1], lsem.at[11], 0)
+    start_dispatch(packed.at[1], gin, asend.at[1], arecv.at[1], lsem.at[11], 1)
+    cots.pass_on(2)
+    cots.far_on(1)
+    cots.pass_on(3)
+    cots.far_on(2)
+    cots.far_on(3)
     for c in loads[8:]:
         c.wait()
 
@@ -402,26 +409,27 @@
             ddown[e, :, cs] = dot(act_s[e], gcot[b, e], 0, 0).astype(BF)
 
     def tview(f, block):
-        t, e, hf = f
-        return t_ref.at[t, block, e, pl.ds(hf * HR, HR)]
+        t, e, q = f
+        return t_ref.at[t, block, e, pl.ds(q * PART, PART)]
+
+    def index(f):
+        return (f[0] * 2 + f[1]) * PARTS + f[2]
 
     def copy(kind, f, block, target):
-        n = f[0] * 4 + f[1] * 2 + f[2]
+        n = index(f)
         return remote(tview(f, block), r_ref.at[n, kind], fs.at[kind, n], fr.at[kind, n], i, target)
 
     def add(f, block, kinds):
-        n = f[0] * 4 + f[1] * 2 + f[2]
-        v = tview(f, block)
-        acc = v[...].astype(F32)
+        acc = tview(f, block)[...].astype(F32)
         for kind in kinds:
-            acc = acc + r_ref[n, kind].astype(F32)
+            acc = acc + r_ref[index(f), kind].astype(F32)
         return acc.astype(BF)
 
     def stage0(f):
         copy(0, f, pfar, xp).start()
         copy(1, f, pup, up).start()
         copy(2, f, pdown, down).start()
-        if f[2] == 0:
+        if f[2] % 2 == 0:
             copy(6, f, down, down).start()
         else:
             copy(5, f, up, up).start()
@@ -429,26 +437,26 @@
     def stage1(f):
         copy(0, f, far, xp).wait_recv()
         tview(f, far)[...] = add(f, far, (0,))
-        copy(3, f, far, up if f[2] == 0 else down).start()
+        copy(3, f, far, up if f[2] % 2 == 0 else down).start()
         copy(1, f, xp, up).wait_recv()
         copy(2, f, xp, up).wait_recv()
         tview(f, xp)[...] = add(f, xp, (1, 2))
         copy(4, f, xp, xp).start()
 
     def stage2(f):
-        block = up if f[2] == 0 else down
+        block = up if f[2] % 2 == 0 else down
         copy(3, f, block, up).wait_recv()
         tview(f, block)[...] = add(f, block, (3,))
-        copy(5 if f[2] == 0 else 6, f, block, block).start()
+        copy(5 if f[2] % 2 == 0 else 6, f, block, block).start()
 
     def stage3(f):
-        t, e, hf = f
+        t, e, q = f
         for kind in (4, 5, 6):
             copy(kind, f, h, up).wait_recv()
-        fin[t, e, hf * HR : (hf + 1) * HR] = add(f, h, (4, 5, 6))
+        fin[t, e, q * PART : (q + 1) * PART] = add(f, h, (4, 5, 6))
 
         def send(k, c):
-            d = hf * 16 + k
+            d = q * (PART // CAP) + k
 
             @pl.when(d != i)
             def _():
@@ -456,7 +464,7 @@
 
             return c
 
-        lax.fori_loop(0, 16, send, 0)
+        lax.fori_loop(0, PART // CAP, send, 0)
 
     def back(t, e, d):
         return remote(fin.at[t, e, pl.ds(pl.multiple_of(d * CAP, CAP), CAP)], picked.at[t, e, i],
@@ -466,7 +474,8 @@
         for kind, block in ((0, pfar), (1, pup), (2, pdown), (3, far), (4, xp), (5, up), (6, down)):
             copy(kind, f, block, xp).wait_send()
 
-    flows = [(t, e, hf) for t in range(2) for e in range(2) for hf in range(2)]
+    flows = [(t, e, q) for t in range(2) for e in range(2) for q in range(PARTS)]
+    count = len(flows)
     outward = [
         pltpu.make_async_copy(s, d, osem.at[n])
         for n, (s, d) in enumerate((
@@ -474,30 +483,6 @@
             (dgate, dgate_out), (dup, dup_out), (ddown, ddown_out),
         ))
     ]
-
-    def tick(n):
-        if n < len(flows):
-            t, e, hf = flows[n]
-            (forward if t == 0 else backward)(e, hf)
-            stage0(flows[n])
-        elif n == len(flows):
-            weight_grads(0)
-        elif n == len(flows) + 1:
-            weight_grads(1)
-            for c in outward[5:]:
-                c.start()
-        if 0 <= n - 1 < len(flows):
-            stage1(flows[n - 1])
-        if 0 <= n - 2 < len(flows):
-            stage2(flows[n - 2])
-        if 0 <= n - 3 < len(flows):
-            stage3(flows[n - 3])
-
-    for _ in gather_flow(gin, lambda e: dispatched(packed.at[1], gin, asend.at[1], arecv.at[1], e).wait_recv(),
-                         gs.at[1], gr.at[1], tick):
-        pass
-    for n in range(4, len(flows) + 3):
-        tick(n)
 
     def landed(t):
         mine = pl.ds(pl.multiple_of(i * CAP, CAP), CAP)
@@ -509,15 +494,63 @@
             remote(part, part, bs.at[t, e], br.at[t, e], i, xp).wait()
         return picked[t].reshape(SLOTS, W)
 
-    rows = landed(0)
-    moe[...] = (dot(whi[...], rows) + dot(wlo[...], rows)).astype(BF)
-    outward[0].start()
-    every = dot(cot_ref[...], rows, 1, 1) * place[...].astype(F32)
-    n = lax.broadcasted_iota(jnp.int32, (TOK, SLOTS), 1)
-    expert = 2 * (lax.rem(n, ROWS) // CAP) + n // ROWS
-    columns = [
-        jnp.sum(jnp.where(expert == ids[:, k : k + 1], every, 0.0), axis=1, keepdims=True) for k in range(TOP)
-    ]
+    def combine():
+        rows = landed(0)
+        moe[...] = (dot(whi[...], rows) + dot(wlo[...], rows)).astype(BF)
+        outward[0].start()
+        every = dot(cot_ref[...], rows, 1, 1) * place[...].astype(F32)
+        n = lax.broadcasted_iota(jnp.int32, (TOK, SLOTS), 1)
+        expert = 2 * (lax.rem(n, ROWS) // CAP) + n // ROWS
+        columns = [
+            jnp.sum(jnp.where(expert == ids[:, k : k + 1], every, 0.0), axis=1, keepdims=True) for k in range(TOP)
+        ]
+        return columns
+
+    columns = []
+
+    def tick(n):
+        if n < count:
+            t, e, q = flows[n]
+            (forward if t == 0 else backward)(e, q)
+            stage0(flows[n])
+        if 0 <= n - 1 < count:
+            stage1(flows[n - 1])
+        if 0 <= n - 2 < count:
+            stage2(flows[n - 2])
+        if 0 <= n - 3 < count:
+            stage3(flows[n - 3])
+        if n == 3 * PARTS:
+            weight_grads(0)
+        if n == 3 * PARTS + 2:
+            columns.extend(combine())
+
+    ins = HeadGather(gin, gs.at[1], gr.at[1])
+    sent(1, gin, 0).wait_recv()
+    ins.own(0)
+    ins.own(1)
+    ins.pass_on(0)
+    sent(1, gin, 1).wait_recv()
+    ins.own(2)
+    ins.pass_on(1)
+    ins.far_on(0)
+    ins.own(3)
+    ins.pass_on(2)
+    ins.far_on(1)
+    ins.whole(0)
+    tick(0)
+    ins.pass_on(3)
+    ins.far_on(2)
+    ins.whole(1)
+    tick(1)
+    ins.far_on(3)
+    ins.whole(2)
+    tick(2)
+    ins.whole(3)
+    tick(3)
+    for n in range(4):
+        cots.whole(n)
+    for n in range(2 * PARTS, count + 3):
+        tick(n)
 
     rows = landed(1)
     input_grad = dot(place[...], rows)
@@ -552,6 +585,10 @@
         d = lax.rem(h + o, NH)
         remote(rgb.at[h], rgb.at[h], rs.at[o], rr.at[o], i, d).start()
 
+    weight_grads(1)
+    for c in outward[5:]:
+        c.start()
+
     def gain_wait(o, c):
         gain_copy(o).wait()
         return c + gsum[o]
@@ -562,7 +599,9 @@
         drain(f)
     for part in range(2):
         for e in range(2):
-            dispatched(packed.at[part], (gcot, gin)[part], asend.at[part], arecv.at[part], e).wait_send()
+            sent(part, (gcot, gin)[part], e).wait_send()
+    cots.drain()
+    ins.drain()
     q_swap.wait_send()
     o_swap.wait_send()
     s_swap.wait_send()
@@ -605,14 +644,14 @@
             v((NH, 8, TOK), F32), v((NH, 8, TOK), F32), v((TOK, W), F32), v((TOK, TOK), F32),
             v((2, ROWS, FD), BF), v((2, ROWS, FD), BF), v((2, ROWS, FD), BF),
             v((2, ROWS, FD), F32), v((2, ROWS, FD), F32),
-            v((2, NH, 2, ROWS, W), BF), v((8, 7, ROWS // 2, W), BF), v((2, 2, ROWS, W), BF),
+            v((2, NH, 2, ROWS, W), BF), v((4 * PARTS, 7, PART, W), BF), v((2, 2, ROWS, W), BF),
             v((2, 2, NC, CAP, W), BF), v((NH, TOK, W), BF), v((NC, 8, W), F32),
             *[v(s, t) for s, t in RESULTS],
             DMA((12,)), DMA((8,)),
             DMA((2, 2, 4)), DMA((2, 2, 4)), DMA((2, 8)), DMA((2, 8)), DMA((3,)), DMA((3,)),
-            DMA((2, 2)), DMA((2, 2)), DMA((2, 7, 4)), DMA((2, 7, 4)), DMA((NH,)), DMA((NH,)),
+            DMA((2, 2)), DMA((2, 2)), DMA((2, 7, 2 * PARTS)), DMA((2, 7, 2 * PARTS)), DMA((NH,)), DMA((NH,)),
             DMA((2, NH)), DMA((2, NH)),
-            DMA((7, 8)), DMA((7, 8)), DMA((2, 2)), DMA((2, 2)), DMA((NH,)), DMA((NH,)), DMA((NC,)), DMA((NC,)),
+            DMA((7, 4 * PARTS)), DMA((7, 4 * PARTS)), DMA((2, 2)), DMA((2, 2)), DMA((NH,)), DMA((NH,)), DMA((NC,)), DMA((NC,)),
         ],
         compiler_params=pltpu.CompilerParams(collective_id=1, has_side_effects=True, vmem_limit_bytes=60 << 20),
         name="layer",

time: 199 us -> 192 us (0.965)
  Pallas kernels: 197 us -> 189 us
    pallas_call x1, Pallas kernels: 193 us -> 185 us  [call_layer(): pl.pallas_call(layer_kernel, out_shape=tuple((SDS(s, t) for s, t in RESUL...]
where the time goes in v3:
time: 192 us; the launch traced here: 190 us
  Pallas kernels  189 us (98%)
    pallas_call x1, Pallas kernels, call_layer(): pl.pallas_call(layer_kernel, out_shape=tuple((SDS(s, t) for s, t in RESUL...  185 us
    pallas_call x1, Pallas kernels, hand_on(): pl.pallas_call(kernel, out_shape=tuple((SDS(s, t) for s, t in RESULTS)),...  3.99 us

profile of v3, /device:TPU:2, one launch (start us, length us, event | category | flops | bytes accessed | tf_op | source)
XLA Modules:
  0.0 189.8 jit_solution(13033306382154008798)
XLA Ops:
  0.6 185.0 %layer.1 = (bf16[128,256]{1,0:T(8,128)(2,1)}, bf16[128,256]{1,0:T(8,128)(2,1)}, bf16[128,256]{1,0:T(8,128)(2,1)}, f32[1,256]{1,0:T(1,128)}, f32[6,128]{1,0:T(8,1...) custom-call(bf16[128,256]{1,0:T(8,128)(2,1)} %q_in.1, ...), custom_call_target="tpu_custom_call" | custom-call | tf_op jit(solution)/shard_map/layer/pallas_call | solution.py:632
  185.6 4.0 %hand_on.1 = (bf16[128,256]{1,0:T(8,128)(2,1)}, bf16[128,256]{1,0:T(8,128)(2,1)}, bf16[128,256]{1,0:T(8,128)(2,1)}, f32[1,256]{1,0:T(1,128)}, f32[6,128]{1,0:T(8...) custom-call(bf16[128,256]{1,0:T(8,128)(2,1)} %get-tuple-element.24.refs_0_, ...), custom_call_target="tpu_custom_call" | custom-call | tf_op jit(solution)/shard_map/hand_on/pallas_call | solution.py:680

commit v4 on v3

--- a/solution.py
+++ b/solution.py
@@ -366,8 +366,6 @@
     cots.pass_on(2)
     cots.far_on(1)
     cots.pass_on(3)
-    cots.far_on(2)
-    cots.far_on(3)
     for c in loads[8:]:
         c.wait()
 
@@ -506,8 +504,6 @@
         ]
         return columns
 
-    columns = []
-
     def tick(n):
         if n < count:
             t, e, q = flows[n]
@@ -519,15 +515,13 @@
             stage2(flows[n - 2])
         if 0 <= n - 3 < count:
             stage3(flows[n - 3])
-        if n == 3 * PARTS:
-            weight_grads(0)
-        if n == 3 * PARTS + 2:
-            columns.extend(combine())
 
     ins = HeadGather(gin, gs.at[1], gr.at[1])
     sent(1, gin, 0).wait_recv()
     ins.own(0)
+    cots.far_on(2)
     ins.own(1)
+    cots.far_on(3)
     ins.pass_on(0)
     sent(1, gin, 1).wait_recv()
     ins.own(2)
@@ -552,6 +546,7 @@
     for n in range(2 * PARTS, count + 3):
         tick(n)
 
+    columns = combine()
     rows = landed(1)
     input_grad = dot(place[...], rows)
     nrm = normed[...]
@@ -585,6 +580,7 @@
         d = lax.rem(h + o, NH)
         remote(rgb.at[h], rgb.at[h], rs.at[o], rr.at[o], i, d).start()
 
+    weight_grads(0)
     weight_grads(1)
     for c in outward[5:]:
         c.start()

time: 192 us -> 189 us (0.984)
  Pallas kernels: 189 us -> 186 us
    pallas_call x1, Pallas kernels: 185 us -> 182 us  [call_layer(): pl.pallas_call(layer_kernel, out_shape=tuple((SDS(s, t) for s, t in RESUL...]
where the time goes in v4:
time: 189 us; the launch traced here: 187 us
  Pallas kernels  186 us (98%)
    pallas_call x1, Pallas kernels, call_layer(): pl.pallas_call(layer_kernel, out_shape=tuple((SDS(s, t) for s, t in RESUL...  182 us
    pallas_call x1, Pallas kernels, hand_on(): pl.pallas_call(kernel, out_shape=tuple((SDS(s, t) for s, t in RESULTS)),...  3.99 us

profile of v4, /device:TPU:2, one launch (start us, length us, event | category | flops | bytes accessed | tf_op | source)
XLA Modules:
  0.0 186.8 jit_solution(10560490106071043136)
XLA Ops:
  0.6 182.0 %layer.1 = (bf16[128,256]{1,0:T(8,128)(2,1)}, bf16[128,256]{1,0:T(8,128)(2,1)}, bf16[128,256]{1,0:T(8,128)(2,1)}, f32[1,256]{1,0:T(1,128)}, f32[6,128]{1,0:T(8,1...) custom-call(bf16[128,256]{1,0:T(8,128)(2,1)} %q_in.1, ...), custom_call_target="tpu_custom_call" | custom-call | tf_op jit(solution)/shard_map/layer/pallas_call | solution.py:628
  182.7 4.0 %hand_on.1 = (bf16[128,256]{1,0:T(8,128)(2,1)}, bf16[128,256]{1,0:T(8,128)(2,1)}, bf16[128,256]{1,0:T(8,128)(2,1)}, f32[1,256]{1,0:T(1,128)}, f32[6,128]{1,0:T(8...) custom-call(bf16[128,256]{1,0:T(8,128)(2,1)} %get-tuple-element.24.refs_0_, ...), custom_call_target="tpu_custom_call" | custom-call | tf_op jit(solution)/shard_map/hand_on/pallas_call | solution.py:676
